TPU v7x, 32 devices: a whole 2x2x4 slice. The times are simulated.
32 devices in a mesh: dp: 2 (over x), expert: 16 (over z, y, core).
Axes of the slice: x: 2, y: 2, z: 4, core: 2. Of those that a mesh axis runs over, the one named last changes fastest.
Arguments:
- tokens: bfloat16 [256, 2048], P('expert', 'dp'), may hold values from -6 to 6
- cotangent: bfloat16 [256, 2048], P('expert', 'dp'), may hold values from -6 to 6
- expert_ids: int32 [256, 8], P('expert'), may hold values from 0 to 15, all different within a row; in each aligned block of 16 rows (0 to 15, 16 to 31, ...) at most 16 rows name the same one
- gate_probs: float32 [256, 8], P('expert'), may hold values from 0.05 to 1
- w_gate: bfloat16 [16, 768, 2048], P('expert', None, 'dp'), may hold values from -0.125 to 0.125
- w_up: bfloat16 [16, 768, 2048], P('expert', None, 'dp'), may hold values from -0.125 to 0.125
- w_down: bfloat16 [16, 768, 2048], P('expert', None, 'dp'), may hold values from -0.21875 to 0.21875
Outputs:
- mixed: bfloat16 [256, 2048], P('expert', 'dp')
- grad_tokens: bfloat16 [256, 2048], P('expert', 'dp')
- grad_gate: bfloat16 [16, 768, 2048], P('expert', None, 'dp')
- grad_up: bfloat16 [16, 768, 2048], P('expert', None, 'dp')
- grad_down: bfloat16 [16, 768, 2048], P('expert', None, 'dp')
Inputs may be any that keep to these rules, and one draw needn't show every extreme that they name: `expert_ids`: each token names 8 different experts. The 16 tokens of one index of expert (rows b * 16 to (b + 1) * 16 - 1) name no expert more than 16 times, a bound that some block reaches.
All inputs are finite; a program needn't handle non-finite values.
Results may differ from a plain program's by a relative error of at most 0.02.
Values may be sent and summed in bfloat16 or wider, within the bound.
No kernel may reach another device: no remote copies, remote signals or barrier semaphores. Data moves between devices by JAX's collectives and lax.ppermute only.
A program may use at most 64 MiB of HBM per device.

v0:
```python
import jax
import jax.numpy as jnp
from jax import lax
from jax.sharding import PartitionSpec as P


def activate(pre_gate, pre_up, back_hidden):
    sigmas = jax.nn.sigmoid(pre_gate)
    silu_vals = pre_gate * sigmas
    hidden = (silu_vals * pre_up).astype(jnp.bfloat16)
    back_gate = (back_hidden * pre_up * sigmas * (1.0 + pre_gate * (1.0 - sigmas))).astype(
        jnp.bfloat16
    )
    back_up = (back_hidden * silu_vals).astype(jnp.bfloat16)
    return (hidden, back_gate, back_up)


def deliver(outbound):
    return lax.all_to_all(outbound, "expert", split_axis=0, concat_axis=0, tiled=True)


def on_device(tokens, cotangent, expert_ids, gate_probs, w_gate, w_up, w_down):
    tok_rows, columns = tokens.shape
    top_count = expert_ids.shape[1]
    experts = lax.axis_size("expert")
    capacity = min(tok_rows, max(2, 2 * tok_rows * top_count // experts))
    slot_count = experts * capacity
    flat_ids = expert_ids.reshape(-1)
    onehot = (flat_ids[:, None] == jnp.arange(experts, dtype=jnp.int32)[None, :]).astype(jnp.int32)
    before = jnp.cumsum(onehot, axis=0) - onehot
    ranks = jnp.sum(before * onehot, axis=1)
    slot_ids = flat_ids * capacity + ranks
    chosen = (slot_ids[:, None] == jnp.arange(slot_count, dtype=jnp.int32)[None, :]).astype(
        jnp.float32
    )
    chosen = chosen.reshape(tok_rows, top_count, slot_count)
    select = jnp.sum(chosen, axis=1)
    weighted = jnp.sum(chosen * gate_probs[:, :, None], axis=1)
    contract_rows = (((0,), (0,)), ((), ()))
    contract_cols = (((1,), (1,)), ((), ()))
    x_rows = lax.dot_general(
        select.astype(jnp.bfloat16), tokens, contract_rows, preferred_element_type=jnp.float32
    ).astype(jnp.bfloat16)
    back_row = lax.dot_general(
        weighted,
        cotangent.astype(jnp.float32),
        contract_rows,
        precision=lax.Precision.HIGHEST,
        preferred_element_type=jnp.float32,
    ).astype(jnp.bfloat16)
    outbound = jnp.stack([x_rows, back_row], axis=1).reshape(experts, capacity, 2, columns)
    inbound = deliver(outbound).reshape(slot_count, 2, columns)
    x_in = inbound[:, 0]
    d_in = inbound[:, 1]
    gate_mat = w_gate[0]
    up_mat = w_up[0]
    down_mat = w_down[0]
    part_gate = lax.dot_general(x_in, gate_mat, contract_cols, preferred_element_type=jnp.float32)
    part_up = lax.dot_general(x_in, up_mat, contract_cols, preferred_element_type=jnp.float32)
    part_back = lax.dot_general(d_in, down_mat, contract_cols, preferred_element_type=jnp.float32)
    pre_gate, pre_up, back_hidden = (
        lax.psum(part_gate.astype(jnp.bfloat16), "dp").astype(jnp.float32),
        lax.psum(part_up.astype(jnp.bfloat16), "dp").astype(jnp.float32),
        lax.psum(part_back.astype(jnp.bfloat16), "dp").astype(jnp.float32),
    )
    hidden, back_gate, back_up = activate(pre_gate, pre_up, back_hidden)
    expert_out = jnp.dot(hidden, down_mat, preferred_element_type=jnp.float32).astype(jnp.bfloat16)
    back_rows = (
        jnp.dot(back_gate, gate_mat, preferred_element_type=jnp.float32)
        + jnp.dot(back_up, up_mat, preferred_element_type=jnp.float32)
    ).astype(jnp.bfloat16)
    grad_gate = lax.dot_general(
        back_gate, x_in, contract_rows, preferred_element_type=jnp.float32
    ).astype(jnp.bfloat16)
    grad_up = lax.dot_general(
        back_up, x_in, contract_rows, preferred_element_type=jnp.float32
    ).astype(jnp.bfloat16)
    grad_down = lax.dot_general(
        hidden, d_in, contract_rows, preferred_element_type=jnp.float32
    ).astype(jnp.bfloat16)
    homeward = jnp.stack([expert_out, back_rows], axis=1).reshape(experts, capacity, 2, columns)
    returned = deliver(homeward).reshape(slot_count, 2, columns)
    mixed = jnp.dot(
        weighted,
        returned[:, 0].astype(jnp.float32),
        precision=lax.Precision.HIGHEST,
        preferred_element_type=jnp.float32,
    ).astype(jnp.bfloat16)
    grad_tokens = jnp.dot(
        select.astype(jnp.bfloat16), returned[:, 1], preferred_element_type=jnp.float32
    ).astype(jnp.bfloat16)
    return (mixed, grad_tokens, grad_gate[None], grad_up[None], grad_down[None])


def solution(mesh):
    in_specs = (
        P("expert", "dp"),
        P("expert", "dp"),
        P("expert", None),
        P("expert", None),
        P("expert", None, "dp"),
        P("expert", None, "dp"),
        P("expert", None, "dp"),
    )
    out_specs = (
        P("expert", "dp"),
        P("expert", "dp"),
        P("expert", None, "dp"),
        P("expert", None, "dp"),
        P("expert", None, "dp"),
    )
    return jax.shard_map(
        on_device, mesh=mesh, in_specs=in_specs, out_specs=out_specs, check_vma=False
    )
```

profile of v0, /device:TPU:0, one launch (start us, length us, event | category | flops | bytes accessed | tf_op | source)
XLA Modules:
  0.0 136.5 jit_solution(10404317828290039889)
XLA Ops:
  7.2 0.9 copy.34
  8.1 0.1 eq.29
  8.2 0.8 copy.36
  8.9 0.1 fusion.42
  9.0 0.2 reduce_window_sum.11
  9.2 0.2 select_reduce_fusion.1
  9.4 0.1 reduce_sum.30
  9.5 0.2 convert_reduce_fusion
  9.7 1.1 convolution_convert_fusion.4
  10.7 1.4 %convolution_convert_fusion.3 = bf16[256,1024]{1,0:T(8,128)(2,1)S(1)} fusion(f32[16,256]{1,0:T(8,128)S(1)} %get-tuple-element.6, bf16[16,1024]{1,0:T(8,128)(2,1)} %param.8), kind=kOutput, calls=%fused_computation.21 | convolution fusion | flops 50593792 | bytes 573440 | tf_op jit(solution)/shard_map/dot_general | solution.py:44
  12.1 0.1 pad_maximum_fusion
  12.2 32.0 %all_to_all.10 = bf16[16,16,2,1024]{3,1,2,0:T(8,128)(2,1)S(1)} all-to-all(bf16[16,16,2,1024]{3,1,2,0:T(8,128)(2,1)S(1)} %pad_maximum_fusion), channel_id=1, replica_groups=mesh['dp'=2,'expert'=16] {'expert'}, dimensions={0} | all-to-all | bytes 2097152 | tf_op jit(solution)/shard_map/all_to_all | solution.py:19
  44.3 0.1 copy.39
  44.4 1.7 %copy-done.3 = bf16[1,768,1024]{2,1,0:T(8,128)(2,1)S(1)} copy-done((bf16[1,768,1024]{2,1,0:T(8,128)(2,1)S(1)}, bf16[1,768,1024]{2,1,0:T(8,128)(2,1)}, u32[]{:S(2)}) %copy-start.3) | copy-done | bytes 1572888
  46.0 1.4 %fusion.27 = bf16[256,768]{1,0:T(8,128)(2,1)} fusion(bf16[1,768,1024]{2,1,0:T(8,128)(2,1)S(1)} %copy-done.3, bf16[256,2,1024]{2,0,1:T(8,128)(2,1)S(1)} %bitcast.73), kind=kOutput, calls=%fused_computation.24 | convolution fusion | flops 402849792 | bytes 2490368 | tf_op jit(solution)/shard_map/dot_general | solution.py:59
  47.4 1.4 %fusion.30 = bf16[256,768]{1,0:T(8,128)(2,1)} fusion(bf16[1,768,1024]{2,1,0:T(8,128)(2,1)S(1)} %copy-done, bf16[256,2,1024]{2,0,1:T(8,128)(2,1)S(1)} %bitcast.74), kind=kOutput, calls=%fused_computation.25 | convolution fusion | flops 402849792 | bytes 2490368 | tf_op jit(solution)/shard_map/dot_general | solution.py:60
  48.8 1.4 fusion.24
  50.2 43.7 %all-reduce.3.cloned.1.call-done = (bf16[256,768]{1,0:T(8,128)(2,1)}, bf16[256,768]{1,0:T(8,128)(2,1)}, bf16[256,768]{1,0:T(8,128)(2,1)}) async-done(((bf16[256,768]{1,0:T(8,128)(2,1)}, bf16[256,768]{1,0:T(8,128)(2,1)}, bf16[256,768]{1,0:T(8,128)(2,1)}), (bf16[256,768]{1,0:T(8,128)(2,1)}, bf16[256,768]{1,0:T(8,128)(2,1)}, bf16[256,768]{1,0:T(8,128)(2,1)})) %all-reduce.3.cloned.1.call-update) | async-done | bytes 1179664 | tf_op jit(solution)/shard_map/psum | solution.py:64
  94.0 1.9 %fusion.21 = bf16[256,1024]{1,0:T(8,128)(2,1)S(1)} fusion(bf16[1,768,1024]{2,1,0:T(8,128)(2,1)S(1)} %copy-done, bf16[256,768]{1,0:T(8,128)(2,1)} %get-tuple-element.9, bf16[256,768]{1,0:T(8,128)(2,1)} %get-tuple-element.8), kind=kOutput, calls=%fused_computation.20 | convolution fusion | flops 404488192 | bytes 2883584 | tf_op jit(solution)/shard_map/dot_general | solution.py:67
  95.9 0.7 fusion.4
  96.6 0.7 copy-done.6
  97.3 0.1 copy-done.9
  97.4 0.8 fusion.18
  98.2 1.1 pad_maximum_fusion.1
  99.3 5.6 %all-to-all-start.1 = ((bf16[16,16,2,1024]{3,1,2,0:T(8,128)(2,1)}), bf16[16,16,2,1024]{3,1,2,0:T(8,128)(2,1)S(1)}, u32[]{:S(2)}, u32[]{:S(2)}) async-start(bf16[16,16,2,1024]{3,1,2,0:T(8,128)(2,1)} %pad_maximum_fusion.1), calls=%async_computation.1 | async-start | bytes 2097152 | tf_op jit(solution)/shard_map/all_to_all | solution.py:19
  104.9 3.0 %fusion.13 = bf16[1,768,1024]{2,1,0:T(8,128)(2,1)} fusion(bf16[256,2,1024]{2,0,1:T(8,128)(2,1)} %bitcast.76, bf16[256,768]{1,0:T(8,128)(2,1)S(1)} %copy-done.7, bf16[256,768]{1,0:T(8,128)(2,1)S(1)} %copy-done.8), kind=kOutput, calls=%fused_computation.16 | convolution fusion | flops 405012480 | bytes 2883584 | tf_op jit(solution)/shard_map/dot_general | solution.py:75
  107.9 1.9 %fusion.14 = bf16[1,768,1024]{2,1,0:T(8,128)(2,1)} fusion(bf16[256,2,1024]{2,0,1:T(8,128)(2,1)S(1)} %bitcast.77, bf16[256,768]{1,0:T(8,128)(2,1)S(1)} %copy-done.10, bf16[256,768]{1,0:T(8,128)(2,1)S(1)} %copy-done.8), kind=kOutput, calls=%fused_computation.17 | convolution fusion | flops 405012480 | bytes 2883584 | tf_op jit(solution)/shard_map/dot_general | solution.py:78
  109.8 2.0 %fusion.12 = bf16[1,768,1024]{2,1,0:T(8,128)(2,1)} fusion(bf16[256,2,1024]{2,0,1:T(8,128)(2,1)S(1)} %bitcast.78, bf16[256,768]{1,0:T(8,128)(2,1)S(1)} %copy-done.10, bf16[256,768]{1,0:T(8,128)(2,1)S(1)} %copy-done.7, bf16[256,768]{1,0:T(8,128)(2,1)S(1)} %copy-done.8), kind=kOutput, calls=%fused_computation.15 | convolution fusion | flops 405995520 | bytes 3276800 | tf_op jit(solution)/shard_map/dot_general | solution.py:72
  111.9 16.0 %all-to-all-done.1 = bf16[16,16,2,1024]{3,1,2,0:T(8,128)(2,1)S(1)} async-done(((bf16[16,16,2,1024]{3,1,2,0:T(8,128)(2,1)}), bf16[16,16,2,1024]{3,1,2,0:T(8,128)(2,1)S(1)}, u32[]{:S(2)}, u32[]{:S(2)}) %all-to-all-start.1) | async-done | bytes 1048608 | tf_op jit(solution)/shard_map/all_to_all | solution.py:19
  127.9 0.1 copy.42
  128.0 0.9 convolution_convert_fusion.6
  128.9 0.8 convolution_convert_fusion.5
  (22 shorter events, 0.1 us)
Async XLA Ops:
  7.2 40.3 %copy-start = (bf16[1,768,1024]{2,1,0:T(8,128)(2,1)S(1)}, bf16[1,768,1024]{2,1,0:T(8,128)(2,1)}, u32[]{:S(2)}) copy-start(bf16[1,768,1024]{2,1,0:T(8,128)(2,1)} %param.13) | copy-start | bytes 4718596
  7.2 86.8 %all-reduce.3.cloned.1.call-start = ((), (), s32[]{:S(2)}) async-start(), calls=%async_computation.2 | async-start | bytes 2359296 | tf_op jit(solution)/shard_map/psum | solution.py:64
  44.3 1.8 %copy-start.3 = (bf16[1,768,1024]{2,1,0:T(8,128)(2,1)S(1)}, bf16[1,768,1024]{2,1,0:T(8,128)(2,1)}, u32[]{:S(2)}) copy-start(bf16[1,768,1024]{2,1,0:T(8,128)(2,1)} %param.12) | copy-start | bytes 4718596
  44.3 4.5 %copy-start.1 = (bf16[16,16,2,1024]{3,1,0,2:T(8,128)(2,1)}, bf16[16,16,2,1024]{3,1,0,2:T(8,128)(2,1)S(1)}, u32[]{:S(2)}) copy-start(bf16[16,16,2,1024]{3,1,0,2:T(8,128)(2,1)S(1)} %copy.39) | copy-start | bytes 3145732
  47.4 1.4 %copy-start.5 = (bf16[1,768,1024]{2,1,0:T(8,128)(2,1)S(1)}, bf16[1,768,1024]{2,1,0:T(8,128)(2,1)}, u32[]{:S(2)}) copy-start(bf16[1,768,1024]{2,1,0:T(8,128)(2,1)} %param.11) | copy-start | bytes 4718596
  94.0 1.9 %copy-start.4 = (bf16[1,768,1024]{2,1,0:T(8,128)(2,1)S(1)}, bf16[1,768,1024]{2,1,0:T(8,128)(2,1)}, u32[]{:S(2)}) copy-start(bf16[1,768,1024]{2,1,0:T(8,128)(2,1)} %param.12) | copy-start | bytes 4718596
  94.0 1.9 %copy-start.7 = (bf16[256,768]{1,0:T(8,128)(2,1)S(1)}, bf16[256,768]{1,0:T(8,128)(2,1)}, u32[]{:S(2)}) copy-start(bf16[256,768]{1,0:T(8,128)(2,1)} %get-tuple-element.7) | copy-start | bytes 1179652
  94.0 1.9 %copy-start.8 = (bf16[256,768]{1,0:T(8,128)(2,1)S(1)}, bf16[256,768]{1,0:T(8,128)(2,1)}, u32[]{:S(2)}) copy-start(bf16[256,768]{1,0:T(8,128)(2,1)} %get-tuple-element.8) | copy-start | bytes 1179652
  95.9 1.4 %copy-start.6 = (bf16[1,768,1024]{2,1,0:T(8,128)(2,1)S(1)}, bf16[1,768,1024]{2,1,0:T(8,128)(2,1)}, u32[]{:S(2)}) copy-start(bf16[1,768,1024]{2,1,0:T(8,128)(2,1)} %param.11) | copy-start | bytes 4718596
  95.9 1.5 %copy-start.9 = (bf16[256,768]{1,0:T(8,128)(2,1)S(1)}, bf16[256,768]{1,0:T(8,128)(2,1)}, u32[]{:S(2)}) copy-start(bf16[256,768]{1,0:T(8,128)(2,1)} %get-tuple-element.9) | copy-start | bytes 1179652
  99.3 28.6 %all-to-all-start.1 = ((bf16[16,16,2,1024]{3,1,2,0:T(8,128)(2,1)}), bf16[16,16,2,1024]{3,1,2,0:T(8,128)(2,1)S(1)}, u32[]{:S(2)}, u32[]{:S(2)}) async-start(bf16[16,16,2,1024]{3,1,2,0:T(8,128)(2,1)} %pad_maximum_fusion.1), calls=%async_computation.1 | async-start | bytes 2097152 | tf_op jit(solution)/shard_map/all_to_all | solution.py:19
  104.9 3.0 %copy-start.2 = (bf16[16,16,2,1024]{3,1,0,2:T(8,128)(2,1)S(1)}, bf16[16,16,2,1024]{3,1,0,2:T(8,128)(2,1)}, u32[]{:S(2)}) copy-start(bf16[16,16,2,1024]{3,1,0,2:T(8,128)(2,1)} %copy-done.1) | copy-start | bytes 3145732
  104.9 3.0 %copy-start.10 = (bf16[256,768]{1,0:T(8,128)(2,1)S(1)}, bf16[256,768]{1,0:T(8,128)(2,1)}, u32[]{:S(2)}) copy-start(bf16[256,768]{1,0:T(8,128)(2,1)} %get-tuple-element.9) | copy-start | bytes 1179652
Sparse Core Ops, SparseCore 0:
  50.4 43.5 all-reduce.2
where the time goes:
time: 138 us; the launch traced here: 137 us
  waiting for transfers between devices  59.7 us (43%)
  blocking collectives  32 us (23%)
  matrix products  18.6 us (13%)
  between operations  14.2 us (10%)
  starting transfers between devices  5.66 us (4%)
  local copies, waits for them, and re-layouts  4.51 us (3%)
  other arithmetic  1.81 us (1%)
    psum x1, waiting for transfers between devices, on_device(): lax.psum(part_back.astype(jnp.bfloat16), 'dp').astype(jnp.float32)  43.7 us
    all_to_all x1, blocking collectives, deliver(): lax.all_to_all(outbound, 'expert', split_axis=0, concat_axis=0, tiled=True)  32 us
    all_to_all x1, waiting for transfers between devices, deliver(): lax.all_to_all(outbound, 'expert', split_axis=0, concat_axis=0, tiled=True)  16 us
    all_to_all x1, starting transfers between devices, deliver(): lax.all_to_all(outbound, 'expert', split_axis=0, concat_axis=0, tiled=True)  5.62 us
    unnamed x24, local copies, waits for them, and re-layouts  4.17 us
    dot_general x1, matrix products, on_device(): lax.dot_general(back_up, x_in, contract_rows, preferred_element_type=jnp....  3.01 us
  transfers between devices with their start and end apart: 2, of which 2 were waited for; matrix products, arithmetic and copies ran while one was open for 5% of the time, Pallas kernels for 0%

commit v1 on v0

--- a/solution.py
+++ b/solution.py
@@ -1,7 +1,144 @@
+import functools
+
 import jax
 import jax.numpy as jnp
 from jax import lax
+from jax.experimental import pallas as pl
+from jax.experimental.pallas import tpu as pltpu
 from jax.sharding import PartitionSpec as P
+
+VMEM = pl.BlockSpec(memory_space=pltpu.VMEM)
+NT = (((1,), (1,)), ((), ()))
+NN = (((1,), (0,)), ((), ()))
+TN = (((0,), (0,)), ((), ()))
+
+
+def dot(a, b, dims):
+    return lax.dot_general(a, b, dims, preferred_element_type=jnp.float32)
+
+
+def partial_kernel(rows_ref, gate_ref, up_ref, down_ref, out_ref):
+    ff, cols = gate_ref.shape
+    x = rows_ref[:, :cols]
+    d = rows_ref[:, cols : 2 * cols]
+    out_ref[:, :ff] = dot(x, gate_ref[...], NT).astype(out_ref.dtype)
+    out_ref[:, ff : 2 * ff] = dot(x, up_ref[...], NT).astype(out_ref.dtype)
+    out_ref[:, 2 * ff :] = dot(d, down_ref[...], NT).astype(out_ref.dtype)
+
+
+def post_kernel(experts, own_ref, other_ref, rows_ref, pick_ref, gate_ref, up_ref, down_ref, out_ref, act_ref):
+    ff, cols = gate_ref.shape
+    prob = jnp.sum(
+        rows_ref[:, 2 * cols :].astype(jnp.float32) * pick_ref[...], axis=1, keepdims=True
+    )
+    both = own_ref[...].astype(jnp.float32) + other_ref[...].astype(jnp.float32)
+    pre_gate = both[:, :ff]
+    pre_up = both[:, ff : 2 * ff]
+    back_hidden = both[:, 2 * ff :] * prob
+    s = 1.0 / (1.0 + jnp.exp(-pre_gate))
+    silu = pre_gate * s
+    hidden = (silu * pre_up * prob).astype(jnp.bfloat16)
+    back_gate = (back_hidden * pre_up * s * (1.0 + pre_gate * (1.0 - s))).astype(jnp.bfloat16)
+    back_up = (back_hidden * silu).astype(jnp.bfloat16)
+    act_ref[:, :ff] = back_gate
+    act_ref[:, ff : 2 * ff] = back_up
+    act_ref[:, 2 * ff :] = hidden
+    out_ref[:, :cols] = dot(hidden, down_ref[...], NN).astype(out_ref.dtype)
+    out_ref[:, cols:] = (
+        dot(back_gate, gate_ref[...], NN) + dot(back_up, up_ref[...], NN)
+    ).astype(out_ref.dtype)
+
+
+def call(kernel, out, *args, flops=0, **kw):
+    nbytes = sum(a.size * a.dtype.itemsize for a in args)
+    return pl.pallas_call(
+        kernel,
+        out_shape=out,
+        in_specs=[VMEM] * len(args),
+        out_specs=jax.tree.map(lambda _: VMEM, out),
+        compiler_params=pltpu.CompilerParams(vmem_limit_bytes=32 * 2**20),
+        cost_estimate=pl.CostEstimate(flops=flops, bytes_accessed=nbytes, transcendentals=0),
+        **kw,
+    )(*args)
+
+
+def swap(a, bits):
+    n = lax.axis_size("expert")
+    return lax.ppermute(a, "expert", [(i, i ^ bits) for i in range(n)])
+
+
+def dense(tokens, cotangent, expert_ids, gate_probs, w_gate, w_up, w_down, groups):
+    tok, cols = tokens.shape
+    experts = lax.axis_size("expert")
+    ff = w_gate.shape[1]
+    gate, up, down = w_gate[0], w_up[0], w_down[0]
+    tail = -(-3 * experts // 128) * 128
+    onehot = expert_ids[:, :, None] == jnp.arange(experts, dtype=jnp.int32)[None, None, :]
+    table = jnp.sum(jnp.where(onehot, gate_probs[:, :, None], 0.0), axis=1)
+    hi = table.astype(jnp.bfloat16)
+    rest = table - hi.astype(jnp.float32)
+    mid = rest.astype(jnp.bfloat16)
+    low = (rest - mid.astype(jnp.float32)).astype(jnp.bfloat16)
+    fill = jnp.zeros((tok, tail - 3 * experts), jnp.bfloat16)
+    packed = jnp.concatenate([tokens, cotangent, hi, mid, low, fill], axis=1)
+    lane = lax.broadcasted_iota(jnp.int32, (1, tail), 1)
+    pick = ((lane % experts == lax.axis_index("expert")) & (lane < 3 * experts)).astype(jnp.float32)
+
+    pieces = {0: packed}
+    for g in groups:
+        for k in g:
+            if k:
+                pieces[k] = swap(packed, 4 * k)
+    rows = []
+    for g in groups:
+        here = jnp.concatenate([pieces[k] for k in g], axis=0) if len(g) > 1 else pieces[g[0]]
+        both = jnp.concatenate([here, swap(here, 2)], axis=0)
+        rows.append(jnp.concatenate([both, swap(both, 1)], axis=0))
+    parts = []
+    for r in rows:
+        n = r.shape[0]
+        parts.append(
+            call(
+                partial_kernel,
+                jax.ShapeDtypeStruct((n, 3 * ff), jnp.bfloat16),
+                r, gate, up, down,
+                flops=6 * n * ff * cols,
+            )
+        )
+    others = [lax.ppermute(p, "dp", [(0, 1), (1, 0)]) for p in parts]
+    outs, acts = [], []
+    for r, p, o in zip(rows, parts, others):
+        n = r.shape[0]
+        out, act = call(
+            functools.partial(post_kernel, experts),
+            (
+                jax.ShapeDtypeStruct((n, 2 * cols), jnp.bfloat16),
+                jax.ShapeDtypeStruct((n, 3 * ff), jnp.bfloat16),
+            ),
+            p, o, r, pick, gate, up, down,
+            flops=6 * n * ff * cols,
+        )
+        outs.append(out)
+        acts.append(act)
+    total = None
+    for g, out in zip(groups, outs):
+        n = out.shape[0]
+        half = out[: n // 2].astype(jnp.float32) + swap(out[n // 2 :], 1).astype(jnp.float32)
+        half = half.astype(jnp.bfloat16)
+        quarter = half[: n // 4].astype(jnp.float32) + swap(half[n // 4 :], 2).astype(jnp.float32)
+        for j, k in enumerate(g):
+            mine = quarter[j * tok : (j + 1) * tok]
+            if k:
+                mine = swap(mine.astype(jnp.bfloat16), 4 * k).astype(jnp.float32)
+            total = mine if total is None else total + mine
+    total = total.astype(jnp.bfloat16)
+    x_all = jnp.concatenate([r[:, :cols] for r in rows], axis=0)
+    d_all = jnp.concatenate([r[:, cols : 2 * cols] for r in rows], axis=0)
+    a_all = jnp.concatenate(acts, axis=0)
+    gg = dot(a_all[:, :ff], x_all, TN).astype(jnp.bfloat16)
+    gu = dot(a_all[:, ff : 2 * ff], x_all, TN).astype(jnp.bfloat16)
+    gd = dot(a_all[:, 2 * ff :], d_all, TN).astype(jnp.bfloat16)
+    return total[:, :cols], total[:, cols:], gg[None], gu[None], gd[None]
 
 
 def activate(pre_gate, pre_up, back_hidden):
@@ -19,7 +156,7 @@
     return lax.all_to_all(outbound, "expert", split_axis=0, concat_axis=0, tiled=True)
 
 
-def on_device(tokens, cotangent, expert_ids, gate_probs, w_gate, w_up, w_down):
+def slotted(tokens, cotangent, expert_ids, gate_probs, w_gate, w_up, w_down):
     tok_rows, columns = tokens.shape
     top_count = expert_ids.shape[1]
     experts = lax.axis_size("expert")
@@ -92,6 +229,16 @@
     return (mixed, grad_tokens, grad_gate[None], grad_up[None], grad_down[None])
 
 
+def on_device(tokens, cotangent, expert_ids, gate_probs, w_gate, w_up, w_down):
+    tok_rows = tokens.shape[0]
+    top_count = expert_ids.shape[1]
+    experts = lax.axis_size("expert")
+    args = (tokens, cotangent, expert_ids, gate_probs, w_gate, w_up, w_down)
+    if 2 * tok_rows * top_count >= experts * tok_rows and experts == 16 and lax.axis_size("dp") == 2:
+        return dense(*args, groups=((0,), (1,), (2, 3)))
+    return slotted(*args)
+
+
 def solution(mesh):
     in_specs = (
         P("expert", "dp"),

time: 138 us -> 71.7 us (0.52)
  blocking collectives: 32 us -> 0 us
  waiting for transfers between devices: 59.7 us -> 29.6 us
  starting transfers between devices: 5.66 us -> 21.2 us
  matrix products: 18.6 us -> 5.24 us
  between operations: 14.2 us -> 1.01 us
  Pallas kernels: 0 us -> 7.79 us
  local copies, waits for them, and re-layouts: 4.51 us -> 6.19 us
    psum x1 -> x0, waiting for transfers between devices: 43.7 us -> none  [on_device(): lax.psum(part_back.astype(jnp.bfloat16), 'dp').astype(jnp.float32)]
    all_to_all x1 -> x0, blocking collectives: 32 us -> none  [deliver(): lax.all_to_all(outbound, 'expert', split_axis=0, concat_axis=0, tiled=True)]
    ppermute x0 -> x21, waiting for transfers between devices: none -> 29.6 us  [the longest x18 17.1 us: swap(): return lax.ppermute(a, 'expert', [(i, i ^ bits) for i in range(n)])]
    ppermute x0 -> x21, starting transfers between devices: none -> 21.2 us  [the longest x18 17.2 us: swap(): return lax.ppermute(a, 'expert', [(i, i ^ bits) for i in range(n)])]
    all_to_all x1 -> x0, waiting for transfers between devices: 16 us -> none  [deliver(): lax.all_to_all(outbound, 'expert', split_axis=0, concat_axis=0, tiled=True)]
    dot_general x13 -> x3, matrix products: 18.6 us -> 5.24 us  [dot(): return lax.dot_general(a, b, dims, preferred_element_type=jnp.float32)]
    pallas_call x0 -> x6, Pallas kernels: none -> 7.79 us  [call(): pl.pallas_call(kernel, out_shape=out, in_specs=[VMEM] * len(args), out_sp...]
    all_to_all x1 -> x0, starting transfers between devices: 5.62 us -> none  [deliver(): lax.all_to_all(outbound, 'expert', split_axis=0, concat_axis=0, tiled=True)]
  transfers between devices with their start and end apart: 2 -> 21, of which waited for: 2 -> 10; matrix products, arithmetic and copies ran while one was open for 5% -> 8% of each run, Pallas kernels for 0% -> 11%
where the time goes in v1:
time: 71.7 us; the launch traced here: 71.4 us
  waiting for transfers between devices  29.6 us (41%)
  starting transfers between devices  21.2 us (30%)
  Pallas kernels  7.79 us (11%)
  local copies, waits for them, and re-layouts  6.19 us (9%)
  matrix products  5.24 us (7%)
  between operations  1.01 us (1%)
    ppermute x18, starting transfers between devices, swap(): return lax.ppermute(a, 'expert', [(i, i ^ bits) for i in range(n)])  17.2 us
    ppermute x18, waiting for transfers between devices, swap(): return lax.ppermute(a, 'expert', [(i, i ^ bits) for i in range(n)])  17.1 us
    ppermute x3, waiting for transfers between devices, dense(): others = [lax.ppermute(p, 'dp', [(0, 1), (1, 0)]) for p in parts]  12.5 us
    pallas_call x6, Pallas kernels, call(): pl.pallas_call(kernel, out_shape=out, in_specs=[VMEM] * len(args), out_sp...  7.79 us
    dot_general x3, matrix products, dot(): return lax.dot_general(a, b, dims, preferred_element_type=jnp.float32)  5.24 us
    unnamed x19, local copies, waits for them, and re-layouts  4.44 us
    ppermute x3, starting transfers between devices, dense(): others = [lax.ppermute(p, 'dp', [(0, 1), (1, 0)]) for p in parts]  3.93 us
  transfers between devices with their start and end apart: 21, of which 10 were waited for; matrix products, arithmetic and copies ran while one was open for 8% of the time, Pallas kernels for 11%

profile of v1, /device:TPU:0, one launch (start us, length us, event | category | flops | bytes accessed | tf_op | source)
XLA Modules:
  0.0 71.4 jit_solution(603866083385336560)
XLA Ops:
  0.6 0.8 %copy.14 = s32[16,8]{1,0:T(8,128)S(1)} copy(s32[16,8]{0,1:T(8,128)} %param.9) | data formatting | bytes 1024 | tf_op args[2]
  1.4 0.8 %copy.15 = f32[16,8]{1,0:T(8,128)S(1)} copy(f32[16,8]{0,1:T(8,128)} %param.10) | data formatting | bytes 1024 | tf_op args[3]
  2.3 0.9 %concatenate.37 = bf16[16,2176]{1,0:T(8,128)(2,1)S(1)} concatenate(bf16[16,1024]{1,0:T(8,128)(2,1)} %param.7, bf16[16,1024]{1,0:T(8,128)(2,1)} %param.8, bf16[16,16]{1,0:T(8,128)(2,1)S(1)} %get-tuple-element.29, bf16[16,16]{1,0:T(8,128)(2,1)S(1)} %get-tuple-element.28, bf16[16,16]{1,0:T(8,128)(2,1)S(1)} %get-tuple-element.27, bf16[16,80]{1,0:T(8,128)(2,1)S(1)} %broadcast_in_dim.29), dimensions={1} | concatenate | bytes 139264 | tf_op jit(solution)/shard_map/concatenate | solution.py:83
  3.2 5.1 %collective-permute-start.13 = (bf16[16,2176]{1,0:T(8,128)(2,1)S(1)}, bf16[16,2176]{1,0:T(8,128)(2,1)S(1)}, u32[]{:S(2)}, u32[]{:S(2)}) collective-permute-start(bf16[16,2176]{1,0:T(8,128)(2,1)S(1)} %concatenate.37), channel_id=1, source_target_pairs={{0,12},{1,13},{2,14},{3,15},{4,8},{5,9},{6,10},{7,11},{8,4},{9,5},... | collective-permute-start | bytes 208904 | tf_op jit(solution)/shard_map/ppermute | solution.py:67
  8.9 1.7 %collective-permute-start = (bf16[16,2176]{1,0:T(8,128)(2,1)S(1)}, bf16[16,2176]{1,0:T(8,128)(2,1)S(1)}, u32[]{:S(2)}, u32[]{:S(2)}) collective-permute-start(bf16[16,2176]{1,0:T(8,128)(2,1)S(1)} %concatenate.37), channel_id=1, source_target_pairs={{0,2},{1,3},{2,0},{3,1},{4,6},{5,7},{6,4},{7,5},{8,10},{9,11},{10,... | collective-permute-start | bytes 208904 | tf_op jit(solution)/shard_map/ppermute | solution.py:67
  10.9 3.2 %collective-permute-done.12 = bf16[16,2176]{1,0:T(8,128)(2,1)S(1)} collective-permute-done((bf16[16,2176]{1,0:T(8,128)(2,1)S(1)}, bf16[16,2176]{1,0:T(8,128)(2,1)S(1)}, u32[]{:S(2)}, u32[]{:S(2)}) %collective-permute-start.12) | collective-permute-done | bytes 69664 | tf_op jit(solution)/shard_map/ppermute | solution.py:67
  14.2 1.6 %collective-permute-start.14 = (bf16[32,2176]{1,0:T(8,128)(2,1)S(1)}, bf16[32,2176]{1,0:T(8,128)(2,1)S(1)}, u32[]{:S(2)}, u32[]{:S(2)}) collective-permute-start(bf16[32,2176]{1,0:T(8,128)(2,1)S(1)} %pad_maximum_fusion.7), channel_id=1, source_target_pairs={{0,2},{1,3},{2,0},{3,1},{4,6},{5,7},{6,4},{7,5},{8,10},{9,11},{10,... | collective-permute-start | bytes 417800 | tf_op jit(solution)/shard_map/ppermute | solution.py:67
  16.5 4.4 %collective-permute-done.6 = bf16[16,2176]{1,0:T(8,128)(2,1)S(1)} collective-permute-done((bf16[16,2176]{1,0:T(8,128)(2,1)S(1)}, bf16[16,2176]{1,0:T(8,128)(2,1)S(1)}, u32[]{:S(2)}, u32[]{:S(2)}) %collective-permute-start.6) | collective-permute-done | bytes 69664 | tf_op jit(solution)/shard_map/ppermute | solution.py:67
  21.6 1.4 %copy-done.1 = bf16[1,768,1024]{2,1,0:T(8,128)(2,1)S(1)} copy-done((bf16[1,768,1024]{2,1,0:T(8,128)(2,1)S(1)}, bf16[1,768,1024]{2,1,0:T(8,128)(2,1)}, u32[]{:S(2)}) %copy-start.1) | copy-done | bytes 1572888
  23.0 1.4 %copy-done.3 = bf16[1,768,1024]{2,1,0:T(8,128)(2,1)S(1)} copy-done((bf16[1,768,1024]{2,1,0:T(8,128)(2,1)S(1)}, bf16[1,768,1024]{2,1,0:T(8,128)(2,1)}, u32[]{:S(2)}) %copy-start.3) | copy-done | bytes 1572888
  24.4 1.5 %shard_map.110.own_ref = bf16[64,2304]{1,0:T(8,128)(2,1)S(1)} custom-call(bf16[64,2176]{1,0:T(8,128)(2,1)S(1)} %pad_maximum_fusion.1.rows_ref, bf16[768,1024]{1,0:T(8,128)(2,1)S(1)} %bitcast.9, bf16[768,1024]{1,0:T(8,128)(2,1)S(1)} %bitcast.15, bf16[768,1024]{1,0:T(8,128)(2,1)S(1)} %bitcast.21), custom_call_target="tpu_custom_call" | custom-call | flops 301989888 | bytes 4997120 | tf_op jit(solution)/shard_map/pallas_call | solution.py:54
  26.0 1.8 %collective-permute-start.2 = (bf16[64,2304]{1,0:T(8,128)(2,1)S(1)}, bf16[64,2304]{1,0:T(8,128)(2,1)S(1)}, u32[]{:S(2)}, u32[]{:S(2)}) collective-permute-start(bf16[64,2304]{1,0:T(8,128)(2,1)S(1)} %shard_map.110.own_ref), channel_id=1, source_target_pairs={{0,16},{16,0},{1,17},{17,1},{2,18},{18,2},{3,19},{19,3},{4,20},{20... | collective-permute-start | bytes 884744 | tf_op jit(solution)/shard_map/ppermute | solution.py:108
  27.9 1.5 %shard_map.112.own_ref = bf16[64,2304]{1,0:T(8,128)(2,1)S(1)} custom-call(bf16[64,2176]{1,0:T(8,128)(2,1)S(1)} %constant_dynamic-update-slice_fusion.rows_ref, bf16[768,1024]{1,0:T(8,128)(2,1)S(1)} %bitcast.10, bf16[768,1024]{1,0:T(8,128)(2,1)S(1)} %bitcast.16, bf16[768,1024]{1,0:T(8,128)(2,1)S(1)} %bitcast.22), custom_call_target="tpu_custom_call" | custom-call | flops 301989888 | bytes 4997120 | tf_op jit(solution)/shard_map/pallas_call | solution.py:54
  29.9 1.7 %shard_map.114.own_ref = bf16[128,2304]{1,0:T(8,128)(2,1)S(1)} custom-call(bf16[128,2176]{1,0:T(8,128)(2,1)S(1)} %constant_dynamic-update-slice_fusion.3.rows_ref, bf16[768,1024]{1,0:T(8,128)(2,1)S(1)} %bitcast.11, bf16[768,1024]{1,0:T(8,128)(2,1)S(1)} %bitcast.17, bf16[768,1024]{1,0:T(8,128)(2,1)S(1)} %bitcast.23), custom_call_target="tpu_custom_call" | custom-call | flops 603979776 | bytes 5275648 | tf_op jit(solution)/shard_map/pallas_call | solution.py:54
  31.5 1.8 %collective-permute-start.16 = (bf16[128,2304]{1,0:T(8,128)(2,1)S(1)}, bf16[128,2304]{1,0:T(8,128)(2,1)S(1)}, u32[]{:S(2)}, u32[]{:S(2)}) collective-permute-start(bf16[128,2304]{1,0:T(8,128)(2,1)S(1)} %shard_map.114.own_ref), channel_id=1, source_target_pairs={{0,16},{16,0},{1,17},{17,1},{2,18},{18,2},{3,19},{19,3},{4,20},{20... | collective-permute-start | bytes 1769480 | tf_op jit(solution)/shard_map/ppermute | solution.py:108
  33.4 2.6 %collective-permute-done.2.other_ref = bf16[64,2304]{1,0:T(8,128)(2,1)S(1)} collective-permute-done((bf16[64,2304]{1,0:T(8,128)(2,1)S(1)}, bf16[64,2304]{1,0:T(8,128)(2,1)S(1)}, u32[]{:S(2)}, u32[]{:S(2)}) %collective-permute-start.2) | collective-permute-done | bytes 294944 | tf_op jit(solution)/shard_map/ppermute | solution.py:108
  35.9 1.0 %shard_map.111 = (bf16[64,2048]{1,0:T(8,128)(2,1)S(1)}, bf16[64,2304]{1,0:T(8,128)(2,1)S(1)}) custom-call(bf16[64,2304]{1,0:T(8,128)(2,1)S(1)} %shard_map.110.own_ref, bf16[64,2304]{1,0:T(8,128)(2,1)S(1)} %collective-permute-done.2.other_ref, bf16[64,2176]{1,0:T(8,128)(2,1)S(1)} %pad_maximum_fusion.1.rows_ref, f32[1,128]{1,0:T(1,128)S(1)} %and_convert_fusion.pick_ref, ...), custom_call_target="tpu_custom_call" | custom-call | flops 301989888 | bytes 5587456 | tf_op jit(solution)/shard_map/pallas_call | solution.py:54
  37.1 5.2 %collective-permute-done.8.other_ref = bf16[64,2304]{1,0:T(8,128)(2,1)S(1)} collective-permute-done((bf16[64,2304]{1,0:T(8,128)(2,1)S(1)}, bf16[64,2304]{1,0:T(8,128)(2,1)S(1)}, u32[]{:S(2)}, u32[]{:S(2)}) %collective-permute-start.8) | collective-permute-done | bytes 294944 | tf_op jit(solution)/shard_map/ppermute | solution.py:108
  42.2 1.0 %shard_map.113 = (bf16[64,2048]{1,0:T(8,128)(2,1)S(1)}, bf16[64,2304]{1,0:T(8,128)(2,1)S(1)}) custom-call(bf16[64,2304]{1,0:T(8,128)(2,1)S(1)} %shard_map.112.own_ref, bf16[64,2304]{1,0:T(8,128)(2,1)S(1)} %collective-permute-done.8.other_ref, bf16[64,2176]{1,0:T(8,128)(2,1)S(1)} %constant_dynamic-update-slice_fusion.rows_ref, ...), custom_call_target="tpu_custom_call" | custom-call | flops 301989888 | bytes 5587456 | tf_op jit(solution)/shard_map/pallas_call | solution.py:54
  43.4 1.3 %collective-permute-done.9 = bf16[32,2048]{1,0:T(8,128)(2,1)S(1)} collective-permute-done((bf16[32,2048]{1,0:T(8,128)(2,1)S(1)}, bf16[32,2048]{1,0:T(8,128)(2,1)S(1)}, u32[]{:S(2)}, u32[]{:S(2)}) %collective-permute-start.9) | collective-permute-done | bytes 131104 | tf_op jit(solution)/shard_map/ppermute | solution.py:67
  44.7 1.8 %collective-permute-start.10 = (bf16[16,2048]{1,0:T(8,128)(2,1)S(1)}, bf16[16,2048]{1,0:T(8,128)(2,1)S(1)}, u32[]{:S(2)}, u32[]{:S(2)}) collective-permute-start(bf16[16,2048]{1,0:T(8,128)(2,1)S(1)} %slice.105), channel_id=1, source_target_pairs={{0,2},{1,3},{2,0},{3,1},{4,6},{5,7},{6,4},{7,5},{8,10},{9,11},{10,... | collective-permute-start | bytes 196616 | tf_op jit(solution)/shard_map/ppermute | solution.py:67
  47.0 2.1 %collective-permute-done.10 = bf16[16,2048]{1,0:T(8,128)(2,1)S(1)} collective-permute-done((bf16[16,2048]{1,0:T(8,128)(2,1)S(1)}, bf16[16,2048]{1,0:T(8,128)(2,1)S(1)}, u32[]{:S(2)}, u32[]{:S(2)}) %collective-permute-start.10) | collective-permute-done | bytes 65568 | tf_op jit(solution)/shard_map/ppermute | solution.py:67
  49.2 4.8 %collective-permute-done.16.other_ref = bf16[128,2304]{1,0:T(8,128)(2,1)S(1)} collective-permute-done((bf16[128,2304]{1,0:T(8,128)(2,1)S(1)}, bf16[128,2304]{1,0:T(8,128)(2,1)S(1)}, u32[]{:S(2)}, u32[]{:S(2)}) %collective-permute-start.16) | collective-permute-done | bytes 589856 | tf_op jit(solution)/shard_map/ppermute | solution.py:108
  53.9 1.0 %shard_map.115 = (bf16[128,2048]{1,0:T(8,128)(2,1)S(1)}, bf16[128,2304]{1,0:T(8,128)(2,1)S(1)}) custom-call(bf16[128,2304]{1,0:T(8,128)(2,1)S(1)} %shard_map.114.own_ref, bf16[128,2304]{1,0:T(8,128)(2,1)S(1)} %collective-permute-done.16.other_ref, bf16[128,2176]{1,0:T(8,128)(2,1)S(1)} %constant_dynamic-update-slice_fusion.3.rows_ref, ...), custom_call_target="tpu_custom_call" | custom-call | flops 603979776 | bytes 6455808 | tf_op jit(solution)/shard_map/pallas_call | solution.py:54
  55.1 1.7 %fusion.1 = bf16[1,768,1024]{2,1,0:T(8,128)(2,1)} fusion(bf16[256,2304]{1,0:T(8,128)(2,1)S(1)} %constant_dynamic-update-slice_fusion.7, bf16[128,1024]{1,0:T(8,128)(2,1)S(1)} %get-tuple-element.18, bf16[64,1024]{1,0:T(8,128)(2,1)S(1)} %get-tuple-element.22, bf16[64,1024]{1,0:T(8,128)(2,1)S(1)} %get-tuple-element.20), kind=kOutput, calls=%fused_computation.4 | convolution fusion | flops 405012480 | bytes 2490368 | tf_op jit(solution)/shard_map/dot_general | solution.py:17
  57.0 1.8 %collective-permute-start.18 = (bf16[32,2048]{1,0:T(8,128)(2,1)S(1)}, bf16[32,2048]{1,0:T(8,128)(2,1)S(1)}, u32[]{:S(2)}, u32[]{:S(2)}) collective-permute-start(bf16[32,2048]{1,0:T(8,128)(2,1)S(1)} %slice.107), channel_id=1, source_target_pairs={{0,2},{1,3},{2,0},{3,1},{4,6},{5,7},{6,4},{7,5},{8,10},{9,11},{10,... | collective-permute-start | bytes 393224 | tf_op jit(solution)/shard_map/ppermute | solution.py:67
  58.8 1.7 %fusion = bf16[1,768,1024]{2,1,0:T(8,128)(2,1)} fusion(bf16[256,2304]{1,0:T(8,128)(2,1)S(1)} %constant_dynamic-update-slice_fusion.7, bf16[128,1024]{1,0:T(8,128)(2,1)S(1)} %get-tuple-element.18, bf16[64,1024]{1,0:T(8,128)(2,1)S(1)} %get-tuple-element.22, bf16[64,1024]{1,0:T(8,128)(2,1)S(1)} %get-tuple-element.20), kind=kOutput, calls=%fused_computation.3 | convolution fusion | flops 405012480 | bytes 2490368 | tf_op jit(solution)/shard_map/dot_general | solution.py:17
  60.5 2.4 %collective-permute-done.18 = bf16[32,2048]{1,0:T(8,128)(2,1)S(1)} collective-permute-done((bf16[32,2048]{1,0:T(8,128)(2,1)S(1)}, bf16[32,2048]{1,0:T(8,128)(2,1)S(1)}, u32[]{:S(2)}, u32[]{:S(2)}) %collective-permute-start.18) | collective-permute-done | bytes 131104 | tf_op jit(solution)/shard_map/ppermute | solution.py:67
  63.0 1.1 %collective-permute-start.19 = (bf16[16,2048]{1,0:T(8,128)(2,1)S(1)}, bf16[16,2048]{1,0:T(8,128)(2,1)S(1)}, u32[]{:S(2)}, u32[]{:S(2)}) collective-permute-start(bf16[16,2048]{1,0:T(8,128)(2,1)S(1)} %get-tuple-element.23), channel_id=1, source_target_pairs={{0,8},{1,9},{2,10},{3,11},{4,12},{5,13},{6,14},{7,15},{8,0},{9,1},... | collective-permute-start | bytes 196616 | tf_op jit(solution)/shard_map/ppermute | solution.py:67
  64.1 1.6 %collective-permute-start.20 = (bf16[16,2048]{1,0:T(8,128)(2,1)S(1)}, bf16[16,2048]{1,0:T(8,128)(2,1)S(1)}, u32[]{:S(2)}, u32[]{:S(2)}) collective-permute-start(bf16[16,2048]{1,0:T(8,128)(2,1)S(1)} %get-tuple-element.24), channel_id=1, source_target_pairs={{0,12},{1,13},{2,14},{3,15},{4,8},{5,9},{6,10},{7,11},{8,4},{9,5},... | collective-permute-start | bytes 196616 | tf_op jit(solution)/shard_map/ppermute | solution.py:67
  65.7 1.7 %fusion.2 = bf16[1,768,1024]{2,1,0:T(8,128)(2,1)} fusion(bf16[128,1024]{1,0:T(8,128)(2,1)S(1)} %get-tuple-element.17, bf16[64,1024]{1,0:T(8,128)(2,1)S(1)} %get-tuple-element.21, bf16[64,1024]{1,0:T(8,128)(2,1)S(1)} %get-tuple-element.19, bf16[256,2304]{1,0:T(8,128)(2,1)S(1)} %constant_dynamic-update-slice_fusion.7), kind=kOutput, calls=%fused_computation.5 | convolution fusion | flops 405012480 | bytes 2490368 | tf_op jit(solution)/shard_map/dot_general | solution.py:17
  67.5 3.2 %collective-permute-done.19 = bf16[16,2048]{1,0:T(8,128)(2,1)S(1)} collective-permute-done((bf16[16,2048]{1,0:T(8,128)(2,1)S(1)}, bf16[16,2048]{1,0:T(8,128)(2,1)S(1)}, u32[]{:S(2)}, u32[]{:S(2)}) %collective-permute-start.19) | collective-permute-done | bytes 65568 | tf_op jit(solution)/shard_map/ppermute | solution.py:67
  (68 shorter events, 4.8 us)
Async XLA Ops:
  3.2 7.7 %collective-permute-start.13 = (bf16[16,2176]{1,0:T(8,128)(2,1)S(1)}, bf16[16,2176]{1,0:T(8,128)(2,1)S(1)}, u32[]{:S(2)}, u32[]{:S(2)}) collective-permute-start(bf16[16,2176]{1,0:T(8,128)(2,1)S(1)} %concatenate.37), channel_id=1, source_target_pairs={{0,12},{1,13},{2,14},{3,15},{4,8},{5,9},{6,10},{7,11},{8,4},{9,5},... | collective-permute-start | bytes 208904 | tf_op jit(solution)/shard_map/ppermute | solution.py:67
  8.2 5.9 %collective-permute-start.12 = (bf16[16,2176]{1,0:T(8,128)(2,1)S(1)}, bf16[16,2176]{1,0:T(8,128)(2,1)S(1)}, u32[]{:S(2)}, u32[]{:S(2)}) collective-permute-start(bf16[16,2176]{1,0:T(8,128)(2,1)S(1)} %concatenate.37), channel_id=1, source_target_pairs={{0,8},{1,9},{2,10},{3,11},{4,12},{5,13},{6,14},{7,15},{8,0},{9,1},... | collective-permute-start | bytes 208904 | tf_op jit(solution)/shard_map/ppermute | solution.py:67
  8.2 7.6 %collective-permute-start.5 = (bf16[16,2176]{1,0:T(8,128)(2,1)S(1)}, bf16[16,2176]{1,0:T(8,128)(2,1)S(1)}, u32[]{:S(2)}, u32[]{:S(2)}) collective-permute-start(bf16[16,2176]{1,0:T(8,128)(2,1)S(1)} %concatenate.37), channel_id=1, source_target_pairs={{0,4},{1,5},{2,6},{3,7},{4,0},{5,1},{6,2},{7,3},{8,12},{9,13},{10,... | collective-permute-start | bytes 208904 | tf_op jit(solution)/shard_map/ppermute | solution.py:67
  8.9 6.9 %collective-permute-start = (bf16[16,2176]{1,0:T(8,128)(2,1)S(1)}, bf16[16,2176]{1,0:T(8,128)(2,1)S(1)}, u32[]{:S(2)}, u32[]{:S(2)}) collective-permute-start(bf16[16,2176]{1,0:T(8,128)(2,1)S(1)} %concatenate.37), channel_id=1, source_target_pairs={{0,2},{1,3},{2,0},{3,1},{4,6},{5,7},{6,4},{7,5},{8,10},{9,11},{10,... | collective-permute-start | bytes 208904 | tf_op jit(solution)/shard_map/ppermute | solution.py:67
  14.2 7.5 %copy-start = (bf16[1,768,1024]{2,1,0:T(8,128)(2,1)S(1)}, bf16[1,768,1024]{2,1,0:T(8,128)(2,1)}, u32[]{:S(2)}) copy-start(bf16[1,768,1024]{2,1,0:T(8,128)(2,1)} %param.11) | copy-start | bytes 4718596
  14.2 6.8 %collective-permute-start.14 = (bf16[32,2176]{1,0:T(8,128)(2,1)S(1)}, bf16[32,2176]{1,0:T(8,128)(2,1)S(1)}, u32[]{:S(2)}, u32[]{:S(2)}) collective-permute-start(bf16[32,2176]{1,0:T(8,128)(2,1)S(1)} %pad_maximum_fusion.7), channel_id=1, source_target_pairs={{0,2},{1,3},{2,0},{3,1},{4,6},{5,7},{6,4},{7,5},{8,10},{9,11},{10,... | collective-permute-start | bytes 417800 | tf_op jit(solution)/shard_map/ppermute | solution.py:67
  15.8 5.8 %collective-permute-start.1 = (bf16[32,2176]{1,0:T(8,128)(2,1)S(1)}, bf16[32,2176]{1,0:T(8,128)(2,1)S(1)}, u32[]{:S(2)}, u32[]{:S(2)}) collective-permute-start(bf16[32,2176]{1,0:T(8,128)(2,1)S(1)} %pad_maximum_fusion.5), channel_id=1, source_target_pairs={{0,1},{1,0},{2,3},{3,2},{4,5},{5,4},{6,7},{7,6},{8,9},{9,8},{10,11... | collective-permute-start | bytes 417800 | tf_op jit(solution)/shard_map/ppermute | solution.py:67
  15.9 5.0 %collective-permute-start.6 = (bf16[16,2176]{1,0:T(8,128)(2,1)S(1)}, bf16[16,2176]{1,0:T(8,128)(2,1)S(1)}, u32[]{:S(2)}, u32[]{:S(2)}) collective-permute-start(bf16[16,2176]{1,0:T(8,128)(2,1)S(1)} %collective-permute-done.5), channel_id=1, source_target_pairs={{0,2},{1,3},{2,0},{3,1},{4,6},{5,7},{6,4},{7,5},{8,10},{9,11},{10,... | collective-permute-start | bytes 208904 | tf_op jit(solution)/shard_map/ppermute | solution.py:67
  20.9 6.9 %collective-permute-start.7 = (bf16[32,2176]{1,0:T(8,128)(2,1)S(1)}, bf16[32,2176]{1,0:T(8,128)(2,1)S(1)}, u32[]{:S(2)}, u32[]{:S(2)}) collective-permute-start(bf16[32,2176]{1,0:T(8,128)(2,1)S(1)} %pad_maximum_fusion.6), channel_id=1, source_target_pairs={{0,1},{1,0},{2,3},{3,2},{4,5},{5,4},{6,7},{7,6},{8,9},{9,8},{10,11... | collective-permute-start | bytes 417800 | tf_op jit(solution)/shard_map/ppermute | solution.py:67
  21.0 8.8 %collective-permute-start.15 = (bf16[64,2176]{1,0:T(8,128)(2,1)S(1)}, bf16[64,2176]{1,0:T(8,128)(2,1)S(1)}, u32[]{:S(2)}, u32[]{:S(2)}) collective-permute-start(bf16[64,2176]{1,0:T(8,128)(2,1)S(1)} %pad_maximum_fusion.2), channel_id=1, source_target_pairs={{0,1},{1,0},{2,3},{3,2},{4,5},{5,4},{6,7},{7,6},{8,9},{9,8},{10,11... | collective-permute-start | bytes 835592 | tf_op jit(solution)/shard_map/ppermute | solution.py:67
  21.6 1.4 %copy-start.1 = (bf16[1,768,1024]{2,1,0:T(8,128)(2,1)S(1)}, bf16[1,768,1024]{2,1,0:T(8,128)(2,1)}, u32[]{:S(2)}) copy-start(bf16[1,768,1024]{2,1,0:T(8,128)(2,1)} %param.12) | copy-start | bytes 4718596
  23.0 1.4 %copy-start.3 = (bf16[1,768,1024]{2,1,0:T(8,128)(2,1)S(1)}, bf16[1,768,1024]{2,1,0:T(8,128)(2,1)}, u32[]{:S(2)}) copy-start(bf16[1,768,1024]{2,1,0:T(8,128)(2,1)} %param.13) | copy-start | bytes 4718596
  26.0 9.9 %collective-permute-start.2 = (bf16[64,2304]{1,0:T(8,128)(2,1)S(1)}, bf16[64,2304]{1,0:T(8,128)(2,1)S(1)}, u32[]{:S(2)}, u32[]{:S(2)}) collective-permute-start(bf16[64,2304]{1,0:T(8,128)(2,1)S(1)} %shard_map.110.own_ref), channel_id=1, source_target_pairs={{0,16},{16,0},{1,17},{17,1},{2,18},{18,2},{3,19},{19,3},{4,20},{20... | collective-permute-start | bytes 884744 | tf_op jit(solution)/shard_map/ppermute | solution.py:108
  27.8 2.0 %copy-start.2 = (bf16[1,768,1024]{2,1,0:T(8,128)(2,1)S(1)}, bf16[1,768,1024]{2,1,0:T(8,128)(2,1)}, u32[]{:S(2)}) copy-start(bf16[1,768,1024]{2,1,0:T(8,128)(2,1)} %param.12) | copy-start | bytes 4718596
  27.8 2.0 %copy-start.4 = (bf16[1,768,1024]{2,1,0:T(8,128)(2,1)S(1)}, bf16[1,768,1024]{2,1,0:T(8,128)(2,1)}, u32[]{:S(2)}) copy-start(bf16[1,768,1024]{2,1,0:T(8,128)(2,1)} %param.13) | copy-start | bytes 4718596
  29.4 12.8 %collective-permute-start.8 = (bf16[64,2304]{1,0:T(8,128)(2,1)S(1)}, bf16[64,2304]{1,0:T(8,128)(2,1)S(1)}, u32[]{:S(2)}, u32[]{:S(2)}) collective-permute-start(bf16[64,2304]{1,0:T(8,128)(2,1)S(1)} %shard_map.112.own_ref), channel_id=1, source_target_pairs={{0,16},{16,0},{1,17},{17,1},{2,18},{18,2},{3,19},{19,3},{4,20},{20... | collective-permute-start | bytes 884744 | tf_op jit(solution)/shard_map/ppermute | solution.py:108
  31.5 22.4 %collective-permute-start.16 = (bf16[128,2304]{1,0:T(8,128)(2,1)S(1)}, bf16[128,2304]{1,0:T(8,128)(2,1)S(1)}, u32[]{:S(2)}, u32[]{:S(2)}) collective-permute-start(bf16[128,2304]{1,0:T(8,128)(2,1)S(1)} %shard_map.114.own_ref), channel_id=1, source_target_pairs={{0,16},{16,0},{1,17},{17,1},{2,18},{18,2},{3,19},{19,3},{4,20},{20... | collective-permute-start | bytes 1769480 | tf_op jit(solution)/shard_map/ppermute | solution.py:108
  37.0 9.6 %collective-permute-start.3 = (bf16[32,2048]{1,0:T(8,128)(2,1)S(1)}, bf16[32,2048]{1,0:T(8,128)(2,1)S(1)}, u32[]{:S(2)}, u32[]{:S(2)}) collective-permute-start(bf16[32,2048]{1,0:T(8,128)(2,1)S(1)} %slice.78), channel_id=1, source_target_pairs={{0,1},{1,0},{2,3},{3,2},{4,5},{5,4},{6,7},{7,6},{8,9},{9,8},{10,11... | collective-permute-start | bytes 393224 | tf_op jit(solution)/shard_map/ppermute | solution.py:67
  43.3 1.4 %collective-permute-start.9 = (bf16[32,2048]{1,0:T(8,128)(2,1)S(1)}, bf16[32,2048]{1,0:T(8,128)(2,1)S(1)}, u32[]{:S(2)}, u32[]{:S(2)}) collective-permute-start(bf16[32,2048]{1,0:T(8,128)(2,1)S(1)} %slice.82), channel_id=1, source_target_pairs={{0,1},{1,0},{2,3},{3,2},{4,5},{5,4},{6,7},{7,6},{8,9},{9,8},{10,11... | collective-permute-start | bytes 393224 | tf_op jit(solution)/shard_map/ppermute | solution.py:67
  44.7 4.3 %collective-permute-start.10 = (bf16[16,2048]{1,0:T(8,128)(2,1)S(1)}, bf16[16,2048]{1,0:T(8,128)(2,1)S(1)}, u32[]{:S(2)}, u32[]{:S(2)}) collective-permute-start(bf16[16,2048]{1,0:T(8,128)(2,1)S(1)} %slice.105), channel_id=1, source_target_pairs={{0,2},{1,3},{2,0},{3,1},{4,6},{5,7},{6,4},{7,5},{8,10},{9,11},{10,... | collective-permute-start | bytes 196616 | tf_op jit(solution)/shard_map/ppermute | solution.py:67
  46.6 20.9 %collective-permute-start.4 = (bf16[16,2048]{1,0:T(8,128)(2,1)S(1)}, bf16[16,2048]{1,0:T(8,128)(2,1)S(1)}, u32[]{:S(2)}, u32[]{:S(2)}) collective-permute-start(bf16[16,2048]{1,0:T(8,128)(2,1)S(1)} %slice.103), channel_id=1, source_target_pairs={{0,2},{1,3},{2,0},{3,1},{4,6},{5,7},{6,4},{7,5},{8,10},{9,11},{10,... | collective-permute-start | bytes 196616 | tf_op jit(solution)/shard_map/ppermute | solution.py:67
  49.1 18.4 %collective-permute-start.11 = (bf16[16,2048]{1,0:T(8,128)(2,1)S(1)}, bf16[16,2048]{1,0:T(8,128)(2,1)S(1)}, u32[]{:S(2)}, u32[]{:S(2)}) collective-permute-start(bf16[16,2048]{1,0:T(8,128)(2,1)S(1)} %add_convert_fusion.5), channel_id=1, source_target_pairs={{0,4},{1,5},{2,6},{3,7},{4,0},{5,1},{6,2},{7,3},{8,12},{9,13},{10,... | collective-permute-start | bytes 196616 | tf_op jit(solution)/shard_map/ppermute | solution.py:67
  55.0 1.9 %collective-permute-start.17 = (bf16[64,2048]{1,0:T(8,128)(2,1)S(1)}, bf16[64,2048]{1,0:T(8,128)(2,1)S(1)}, u32[]{:S(2)}, u32[]{:S(2)}) collective-permute-start(bf16[64,2048]{1,0:T(8,128)(2,1)S(1)} %slice.86), channel_id=1, source_target_pairs={{0,1},{1,0},{2,3},{3,2},{4,5},{5,4},{6,7},{7,6},{8,9},{9,8},{10,11... | collective-permute-start | bytes 786440 | tf_op jit(solution)/shard_map/ppermute | solution.py:67
  57.0 6.0 %collective-permute-start.18 = (bf16[32,2048]{1,0:T(8,128)(2,1)S(1)}, bf16[32,2048]{1,0:T(8,128)(2,1)S(1)}, u32[]{:S(2)}, u32[]{:S(2)}) collective-permute-start(bf16[32,2048]{1,0:T(8,128)(2,1)S(1)} %slice.107), channel_id=1, source_target_pairs={{0,2},{1,3},{2,0},{3,1},{4,6},{5,7},{6,4},{7,5},{8,10},{9,11},{10,... | collective-permute-start | bytes 393224 | tf_op jit(solution)/shard_map/ppermute | solution.py:67
  63.0 7.7 %collective-permute-start.19 = (bf16[16,2048]{1,0:T(8,128)(2,1)S(1)}, bf16[16,2048]{1,0:T(8,128)(2,1)S(1)}, u32[]{:S(2)}, u32[]{:S(2)}) collective-permute-start(bf16[16,2048]{1,0:T(8,128)(2,1)S(1)} %get-tuple-element.23), channel_id=1, source_target_pairs={{0,8},{1,9},{2,10},{3,11},{4,12},{5,13},{6,14},{7,15},{8,0},{9,1},... | collective-permute-start | bytes 196616 | tf_op jit(solution)/shard_map/ppermute | solution.py:67
  64.1 6.6 %collective-permute-start.20 = (bf16[16,2048]{1,0:T(8,128)(2,1)S(1)}, bf16[16,2048]{1,0:T(8,128)(2,1)S(1)}, u32[]{:S(2)}, u32[]{:S(2)}) collective-permute-start(bf16[16,2048]{1,0:T(8,128)(2,1)S(1)} %get-tuple-element.24), channel_id=1, source_target_pairs={{0,12},{1,13},{2,14},{3,15},{4,8},{5,9},{6,10},{7,11},{8,4},{9,5},... | collective-permute-start | bytes 196616 | tf_op jit(solution)/shard_map/ppermute | solution.py:67

commit v2 on v0

--- a/solution.py
+++ b/solution.py
@@ -1,7 +1,265 @@
+import functools
+
 import jax
 import jax.numpy as jnp
 from jax import lax
+from jax.experimental import pallas as pl
+from jax.experimental.pallas import tpu as pltpu
 from jax.sharding import PartitionSpec as P
+
+VMEM = pl.BlockSpec(memory_space=pltpu.VMEM)
+HBM = pl.BlockSpec(memory_space=pl.ANY)
+NT = (((1,), (1,)), ((), ()))
+NN = (((1,), (0,)), ((), ()))
+TN = (((0,), (0,)), ((), ()))
+
+
+def dot(a, b, dims):
+    return lax.dot_general(a, b, dims, preferred_element_type=jnp.float32)
+
+
+def pack_kernel(experts, x_hbm, d_hbm, ids_hbm, probs_hbm, lane_ref, out_ref, pick_ref, ids_ref, probs_ref, sems):
+    cols = x_hbm.shape[1]
+    top, tok = ids_ref.shape
+    tail = out_ref.shape[1] - 2 * cols
+    copies = [
+        pltpu.make_async_copy(src, dst, sems.at[i])
+        for i, (src, dst) in enumerate(
+            (
+                (ids_hbm, ids_ref),
+                (probs_hbm, probs_ref),
+                (x_hbm, out_ref.at[:, :cols]),
+                (d_hbm, out_ref.at[:, cols : 2 * cols]),
+            )
+        )
+    ]
+    for copy in copies:
+        copy.start()
+    copies[0].wait()
+    copies[1].wait()
+    number = lax.broadcasted_iota(jnp.int32, (experts, tok), 0)
+    table = jnp.zeros((experts, tok), jnp.float32)
+    for k in range(top):
+        table += jnp.where(ids_ref[k : k + 1, :] == number, probs_ref[k : k + 1, :], 0.0)
+    hi = table.astype(jnp.bfloat16).astype(jnp.float32)
+    mid = (table - hi).astype(jnp.bfloat16).astype(jnp.float32)
+    low = table - hi - mid
+    stacked = jnp.concatenate([hi, mid, low], axis=0).astype(jnp.bfloat16)
+    spread = (
+        lax.broadcasted_iota(jnp.int32, (3 * experts, tail), 0)
+        == lax.broadcasted_iota(jnp.int32, (3 * experts, tail), 1)
+    ).astype(jnp.bfloat16)
+    out_ref[:, 2 * cols :] = dot(stacked, spread, TN).astype(jnp.bfloat16)
+    pick_ref[...] = lane_ref[...]
+    copies[2].wait()
+    copies[3].wait()
+
+
+def partial_kernel(count, *refs):
+    rows, weight_refs, outs = refs[:count], refs[count : count + 3], refs[count + 3 :]
+    ff, cols = weight_refs[0].shape
+    for i, w_ref in enumerate(weight_refs):
+        lo = cols if i == 2 else 0
+        side = jnp.concatenate([r[:, lo : lo + cols] for r in rows], axis=0)
+        share = dot(side, w_ref[...], NT).astype(jnp.bfloat16)
+        start = 0
+        for out_ref in outs:
+            size = out_ref.shape[0]
+            out_ref[:, i * ff : (i + 1) * ff] = share[start : start + size]
+            start += size
+
+
+def post_kernel(own_ref, other_ref, here_ref, there_ref, pick_ref, gate_ref, up_ref, down_ref, out_ref, act_ref):
+    ff, cols = gate_ref.shape
+    table = jnp.concatenate([here_ref[:, 2 * cols :], there_ref[:, 2 * cols :]], axis=0)
+    prob = jnp.sum(table.astype(jnp.float32) * pick_ref[...], axis=1, keepdims=True)
+    both = own_ref[...].astype(jnp.float32) + other_ref[...].astype(jnp.float32)
+    pre_gate = both[:, :ff]
+    pre_up = both[:, ff : 2 * ff]
+    back_hidden = both[:, 2 * ff :] * prob
+    s = 1.0 / (1.0 + jnp.exp(-pre_gate))
+    silu = pre_gate * s
+    hidden = (silu * pre_up * prob).astype(jnp.bfloat16)
+    back_gate = (back_hidden * pre_up * s * (1.0 + pre_gate * (1.0 - s))).astype(jnp.bfloat16)
+    back_up = (back_hidden * silu).astype(jnp.bfloat16)
+    act_ref[:, :ff] = back_gate
+    act_ref[:, ff : 2 * ff] = back_up
+    act_ref[:, 2 * ff :] = hidden
+    out_ref[:, :cols] = dot(hidden, down_ref[...], NN).astype(out_ref.dtype)
+    out_ref[:, cols:] = (
+        dot(back_gate, gate_ref[...], NN) + dot(back_up, up_ref[...], NN)
+    ).astype(out_ref.dtype)
+
+
+def grad_kernel(steps, count, *refs):
+    act_refs, row_refs = refs[:count], refs[count:-5]
+    outs, block_ref, sems = refs[-5:-2], refs[-2], refs[-1]
+    ff, cols = outs[0].shape[1:]
+    size = ff // steps
+    copies = []
+    for i, out_hbm in enumerate(outs):
+        lo = cols if i == 2 else 0
+        side = jnp.concatenate([r[:, lo : lo + cols] for r in row_refs], axis=0)
+        for j in range(steps):
+            at = i * ff + j * size
+            act = jnp.concatenate([r[:, at : at + size] for r in act_refs], axis=0)
+            block_ref[at : at + size, :] = dot(act, side, TN).astype(jnp.bfloat16)
+            copy = pltpu.make_async_copy(
+                block_ref.at[at : at + size, :],
+                out_hbm.at[0, j * size : (j + 1) * size, :],
+                sems.at[i * steps + j],
+            )
+            copy.start()
+            copies.append(copy)
+    for copy in copies:
+        copy.wait()
+
+
+def hbm(a):
+    return pltpu.with_memory_space_constraint(a, pltpu.HBM)
+
+
+def near(a):
+    return pltpu.with_memory_space_constraint(a, pltpu.VMEM)
+
+
+def call(kernel, out, *args, flops=0, free=(), far=(), mib=16, **kw):
+    nbytes = sum(a.size * a.dtype.itemsize for a in args)
+    args = [hbm(a) if i in far else a if i in free else near(a) for i, a in enumerate(args)]
+    return pl.pallas_call(
+        kernel,
+        out_shape=jax.tree.map(lambda o: pltpu.VMEM(o.shape, o.dtype), out),
+        in_specs=[HBM if i in far else VMEM for i in range(len(args))],
+        out_specs=jax.tree.map(lambda _: VMEM, out),
+        compiler_params=pltpu.CompilerParams(vmem_limit_bytes=mib * 2**20),
+        cost_estimate=pl.CostEstimate(flops=flops, bytes_accessed=nbytes, transcendentals=0),
+        **kw,
+    )(*args)
+
+
+def grads(acts, rows, ff, cols):
+    steps = ff // 256 if ff % 256 == 0 else 1
+    count = len(acts)
+    n = sum(a.shape[0] for a in acts)
+    shape = jax.ShapeDtypeStruct((1, ff, cols), jnp.bfloat16)
+    return pl.pallas_call(
+        functools.partial(grad_kernel, steps, count),
+        out_shape=(shape,) * 3,
+        in_specs=[VMEM] * (count + len(rows)),
+        out_specs=(HBM,) * 3,
+        scratch_shapes=[
+            pltpu.VMEM((3 * ff, cols), jnp.bfloat16),
+            pltpu.SemaphoreType.DMA((3 * steps,)),
+        ],
+        compiler_params=pltpu.CompilerParams(vmem_limit_bytes=24 * 2**20),
+        cost_estimate=pl.CostEstimate(
+            flops=6 * n * ff * cols, bytes_accessed=6 * ff * cols, transcendentals=0
+        ),
+    )(*map(near, acts), *map(near, rows))
+
+
+def swap(a, bits):
+    n = lax.axis_size("expert")
+    return lax.ppermute(a, "expert", [(i, i ^ bits) for i in range(n)])
+
+
+def dense(tokens, cotangent, expert_ids, gate_probs, w_gate, w_up, w_down):
+    tok, cols = tokens.shape
+    experts = lax.axis_size("expert")
+    top = expert_ids.shape[1]
+    ff = w_gate.shape[1]
+    tail = -(-3 * experts // 128) * 128
+    bf16 = jnp.bfloat16
+    f32 = jnp.float32
+    lane = lax.broadcasted_iota(jnp.int32, (1, tail), 1)
+    pick = ((lane % experts == lax.axis_index("expert")) & (lane < 3 * experts)).astype(f32)
+    own, pick = call(
+        functools.partial(pack_kernel, experts),
+        (jax.ShapeDtypeStruct((tok, 2 * cols + tail), bf16), jax.ShapeDtypeStruct((1, tail), f32)),
+        tokens, cotangent, expert_ids.T, gate_probs.T, pick,
+        far=(0, 1, 2, 3),
+        free=(4,),
+        flops=3 * 10**10,
+        scratch_shapes=[
+            pltpu.VMEM((top, tok), jnp.int32),
+            pltpu.VMEM((top, tok), f32),
+            pltpu.SemaphoreType.DMA((4,)),
+        ],
+    )
+    weights = (w_gate[0], w_up[0], w_down[0])
+
+    def shares_of(rows, sizes):
+        return call(
+            functools.partial(partial_kernel, len(rows)),
+            tuple(jax.ShapeDtypeStruct((n, 3 * ff), bf16) for n in sizes),
+            *rows, *weights,
+            free=tuple(range(len(rows), len(rows) + 3)),
+            flops=6 * sum(sizes) * ff * cols,
+        )
+
+    def other(share):
+        return lax.ppermute(share, "dp", [(0, 1), (1, 0)])
+
+    def post(share, arrived, here, there):
+        n = share.shape[0]
+        return call(
+            post_kernel,
+            (jax.ShapeDtypeStruct((n, 2 * cols), bf16), jax.ShapeDtypeStruct((n, 3 * ff), bf16)),
+            share, arrived, here, there, pick, *weights,
+            free=(4, 5, 6, 7),
+            flops=6 * n * ff * cols,
+        )
+
+    def fold(a, bits):
+        n = a.shape[0] // 2
+        return a[:n].astype(f32) + swap(a[n:].astype(bf16), bits).astype(f32)
+
+    def after(a, *b):
+        return lax.optimization_barrier((a,) + b)[0]
+
+    n = 4 * tok
+    far = range(2, experts // 4)
+    own_core = swap(own, 1)
+    alone = [swap(own, 4 * k) for k in far]
+    here1 = jnp.concatenate([swap(own, 4), swap(own, 6)], axis=0)
+    there1 = swap(here1, 1)
+    (share1,) = shares_of((here1, there1), (n,))
+    other1 = other(share1)
+    beside = swap(jnp.concatenate(alone, axis=0), 2)
+    *alone, beside, _ = lax.optimization_barrier((*alone, beside, share1))
+    here = [
+        jnp.concatenate([a, beside[i * tok : (i + 1) * tok]], axis=0) for i, a in enumerate(alone)
+    ]
+    there = swap(jnp.concatenate(here, axis=0), 1)
+    there = [there[2 * i * tok : 2 * (i + 1) * tok] for i in range(len(here))]
+    shares = shares_of([r for pair in zip(here, there) for r in pair], (n,) * len(here))
+    others = [other(s) for s in shares]
+    own_beside = swap(after(own, *shares), 2)
+    here0 = jnp.concatenate([own, own_beside], axis=0)
+    there0 = jnp.concatenate([own_core, swap(own_beside, 1)], axis=0)
+    (share0,) = shares_of((here0, there0), (n,))
+    other0 = other(share0)
+
+    out1, act1 = post(share1, after(other1, *shares), here1, there1)
+    near = swap(fold(out1, 1).astype(bf16), 4).astype(f32)
+    acts, halves, quarters, back = [], [], [], []
+    for k, share, arrived, h, t in zip(far, shares, others, here, there):
+        out, act = post(share, after(arrived, *halves[-1:]), h, t)
+        halves.append(fold(out, 1).astype(bf16))
+        quarters.append(fold(halves[-1], 2).astype(bf16))
+        back.append(swap(quarters[-1], 4 * k))
+        acts.append(act)
+    out0, act0 = post(share0, after(other0, quarters[0], halves[-1]), here0, there0)
+    total = fold(near + fold(out0, 1), 2)
+    for b in back:
+        total += b.astype(f32)
+    total = total.astype(bf16)
+    gg, gu, gd = grads(
+        (act0, act1, *acts),
+        (here0, there0, here1, there1, *[r for pair in zip(here, there) for r in pair]),
+        ff, cols,
+    )
+    return total[:, :cols], total[:, cols:], gg, gu, gd
 
 
 def activate(pre_gate, pre_up, back_hidden):
@@ -19,7 +277,7 @@
     return lax.all_to_all(outbound, "expert", split_axis=0, concat_axis=0, tiled=True)
 
 
-def on_device(tokens, cotangent, expert_ids, gate_probs, w_gate, w_up, w_down):
+def slotted(tokens, cotangent, expert_ids, gate_probs, w_gate, w_up, w_down):
     tok_rows, columns = tokens.shape
     top_count = expert_ids.shape[1]
     experts = lax.axis_size("expert")
@@ -92,6 +350,18 @@
     return (mixed, grad_tokens, grad_gate[None], grad_up[None], grad_down[None])
 
 
+def on_device(tokens, cotangent, expert_ids, gate_probs, w_gate, w_up, w_down):
+    tok_rows = tokens.shape[0]
+    top_count = expert_ids.shape[1]
+    experts = lax.axis_size("expert")
+    args = (tokens, cotangent, expert_ids, gate_probs, w_gate, w_up, w_down)
+    pairs = experts // 4
+    powers = pairs > 2 and experts & (experts - 1) == 0
+    if 2 * tok_rows * top_count >= experts * tok_rows and powers and lax.axis_size("dp") == 2:
+        return dense(*args)
+    return slotted(*args)
+
+
 def solution(mesh):
     in_specs = (
         P("expert", "dp"),

time: 138 us -> 57.1 us (0.41)
  waiting for transfers between devices: 59.7 us -> 17.8 us
  blocking collectives: 32 us -> 0 us
  starting transfers between devices: 5.66 us -> 24.6 us
  matrix products: 18.6 us -> 0 us
  between operations: 14.2 us -> 0.95 us
  Pallas kernels: 0 us -> 12.5 us
  local copies, waits for them, and re-layouts: 4.51 us -> 0.81 us
  other arithmetic: 1.81 us -> 0.29 us
    psum x1 -> x0, waiting for transfers between devices: 43.7 us -> none  [on_device(): lax.psum(part_back.astype(jnp.bfloat16), 'dp').astype(jnp.float32)]
    all_to_all x1 -> x0, blocking collectives: 32 us -> none  [deliver(): lax.all_to_all(outbound, 'expert', split_axis=0, concat_axis=0, tiled=True)]
    ppermute x0 -> x24, starting transfers between devices: none -> 24.6 us  [the longest x20 19.1 us: swap(): return lax.ppermute(a, 'expert', [(i, i ^ bits) for i in range(n)])]
    dot_general x13 -> x0, matrix products: 18.6 us -> none  [the longest x1 3.01 us: on_device(): lax.dot_general(back_up, x_in, contract_rows, preferred_element_type=jnp....]
    ppermute x0 -> x24, waiting for transfers between devices: none -> 17.8 us  [the longest x20 9.91 us: swap(): return lax.ppermute(a, 'expert', [(i, i ^ bits) for i in range(n)])]
    all_to_all x1 -> x0, waiting for transfers between devices: 16 us -> none  [deliver(): lax.all_to_all(outbound, 'expert', split_axis=0, concat_axis=0, tiled=True)]
    pallas_call x0 -> x9, Pallas kernels: none -> 12.5 us  [the longest x8 9.95 us: call(): pl.pallas_call(kernel, out_shape=jax.tree.map(lambda o: pltpu.VMEM(o.shap...]
    all_to_all x1 -> x0, starting transfers between devices: 5.62 us -> none  [deliver(): lax.all_to_all(outbound, 'expert', split_axis=0, concat_axis=0, tiled=True)]
  transfers between devices with their start and end apart: 2 -> 24, of which waited for: 2 -> 10; matrix products, arithmetic and copies ran while one was open for 5% -> 1% of each run, Pallas kernels for 0% -> 20%
where the time goes in v2:
time: 57.1 us; the launch traced here: 57 us
  starting transfers between devices  24.6 us (43%)
  waiting for transfers between devices  17.8 us (31%)
  Pallas kernels  12.5 us (22%)
  between operations  0.95 us (2%)
  local copies, waits for them, and re-layouts  0.81 us (1%)
    ppermute x20, starting transfers between devices, swap(): return lax.ppermute(a, 'expert', [(i, i ^ bits) for i in range(n)])  19.1 us
    pallas_call x8, Pallas kernels, call(): pl.pallas_call(kernel, out_shape=jax.tree.map(lambda o: pltpu.VMEM(o.shap...  9.95 us
    ppermute x20, waiting for transfers between devices, swap(): return lax.ppermute(a, 'expert', [(i, i ^ bits) for i in range(n)])  9.91 us
    ppermute x4, waiting for transfers between devices, other(): return lax.ppermute(share, 'dp', [(0, 1), (1, 0)])  7.88 us
    ppermute x4, starting transfers between devices, other(): return lax.ppermute(share, 'dp', [(0, 1), (1, 0)])  5.5 us
    pallas_call x1, Pallas kernels, grads(): pl.pallas_call(functools.partial(grad_kernel, steps, count), out_shape=(s...  2.58 us
  transfers between devices with their start and end apart: 24, of which 10 were waited for; matrix products, arithmetic and copies ran while one was open for 1% of the time, Pallas kernels for 20%

profile of v2, /device:TPU:0, one launch (start us, length us, event | category | flops | bytes accessed | tf_op | source)
XLA Modules:
  0.0 57.0 jit_solution(11797306011519913042)
XLA Ops:
  0.7 1.1 %shard_map.110 = (bf16[16,2176]{1,0:T(8,128)(2,1)S(1)}, f32[1,128]{1,0:T(1,128)S(1)}) custom-call(bf16[16,1024]{1,0:T(8,128)(2,1)} %x_hbm.1, bf16[16,1024]{1,0:T(8,128)(2,1)} %d_hbm.1, s32[8,16]{1,0:T(8,128)} %bitcast.26, f32[8,16]{1,0:T(8,128)} %bitcast.27, f32[1,128]{1,0:T(1,128)S(1)} %and_convert_fusion.lane_ref), custom_call_target="tpu_custom_call" | custom-call | flops 30000001024 | bytes 67072 | tf_op jit(solution)/shard_map/pallas_call | solution.py:129
  1.8 5.1 %collective-permute-start.5 = (bf16[16,2176]{1,0:T(8,128)(2,1)S(1)}, bf16[16,2176]{1,0:T(8,128)(2,1)S(1)}, u32[]{:S(2)}, u32[]{:S(2)}) collective-permute-start(bf16[16,2176]{1,0:T(8,128)(2,1)S(1)} %get-tuple-element.36), channel_id=1, source_target_pairs={{0,12},{1,13},{2,14},{3,15},{4,8},{5,9},{6,10},{7,11},{8,4},{9,5},... | collective-permute-start | bytes 208904 | tf_op jit(solution)/shard_map/ppermute | solution.py:163
  6.9 1.7 %collective-permute-start.1 = (bf16[16,2176]{1,0:T(8,128)(2,1)S(1)}, bf16[16,2176]{1,0:T(8,128)(2,1)S(1)}, u32[]{:S(2)}, u32[]{:S(2)}) collective-permute-start(bf16[16,2176]{1,0:T(8,128)(2,1)S(1)} %get-tuple-element.36), channel_id=1, source_target_pairs={{0,6},{1,7},{2,4},{3,5},{4,2},{5,3},{6,0},{7,1},{8,14},{9,15},{10,... | collective-permute-start | bytes 208904 | tf_op jit(solution)/shard_map/ppermute | solution.py:163
  8.6 1.2 %collective-permute-start = (bf16[16,2176]{1,0:T(8,128)(2,1)S(1)}, bf16[16,2176]{1,0:T(8,128)(2,1)S(1)}, u32[]{:S(2)}, u32[]{:S(2)}) collective-permute-start(bf16[16,2176]{1,0:T(8,128)(2,1)S(1)} %get-tuple-element.36), channel_id=1, source_target_pairs={{0,4},{1,5},{2,6},{3,7},{4,0},{5,1},{6,2},{7,3},{8,12},{9,13},{10,... | collective-permute-start | bytes 208904 | tf_op jit(solution)/shard_map/ppermute | solution.py:163
  9.9 3.0 %collective-permute-done.4 = bf16[16,2176]{1,0:T(8,128)(2,1)S(1)} collective-permute-done((bf16[16,2176]{1,0:T(8,128)(2,1)S(1)}, bf16[16,2176]{1,0:T(8,128)(2,1)S(1)}, u32[]{:S(2)}, u32[]{:S(2)}) %collective-permute-start.4) | collective-permute-done | bytes 69664 | tf_op jit(solution)/shard_map/ppermute | solution.py:163
  12.9 1.6 %collective-permute-start.6 = (bf16[32,2176]{1,0:T(8,128)(2,1)S(1)}, bf16[32,2176]{1,0:T(8,128)(2,1)S(1)}, u32[]{:S(2)}, u32[]{:S(2)}) collective-permute-start(bf16[32,2176]{1,0:T(8,128)(2,1)S(1)} %pad_maximum_fusion.1), channel_id=1, source_target_pairs={{0,2},{1,3},{2,0},{3,1},{4,6},{5,7},{6,4},{7,5},{8,10},{9,11},{10,... | collective-permute-start | bytes 417800 | tf_op jit(solution)/shard_map/ppermute | solution.py:163
  14.5 0.7 %collective-permute-done = bf16[16,2176]{1,0:T(8,128)(2,1)S(1)} collective-permute-done((bf16[16,2176]{1,0:T(8,128)(2,1)S(1)}, bf16[16,2176]{1,0:T(8,128)(2,1)S(1)}, u32[]{:S(2)}, u32[]{:S(2)}) %collective-permute-start) | collective-permute-done | bytes 69664 | tf_op jit(solution)/shard_map/ppermute | solution.py:163
  15.4 1.3 %collective-permute-done.2.refs_1_.there_ref.refs_7_ = bf16[32,2176]{1,0:T(8,128)(2,1)S(1)} collective-permute-done((bf16[32,2176]{1,0:T(8,128)(2,1)S(1)}, bf16[32,2176]{1,0:T(8,128)(2,1)S(1)}, u32[]{:S(2)}, u32[]{:S(2)}) %collective-permute-start.2) | collective-permute-done | bytes 139296 | tf_op jit(solution)/shard_map/ppermute | solution.py:163
  16.7 1.5 %shard_map.111.own_ref = bf16[64,2304]{1,0:T(8,128)(2,1)S(1)} custom-call(bf16[32,2176]{1,0:T(8,128)(2,1)S(1)} %constant_dynamic-update-slice_fusion.refs_0_.here_ref.refs_6_, bf16[32,2176]{1,0:T(8,128)(2,1)S(1)} %collective-permute-done.2.refs_1_.there_ref.refs_7_, bf16[768,1024]{1,0:T(8,128)(2,1)S(1)} %bitcast.5, bf16[768,1024]{1,0:T(8,128)(2,1)S(1)} %bitcast.12, ...), custom_call_target="tpu_custom_call" | custom-call | flops 301989888 | bytes 4997120 | tf_op jit(solution)/shard_map/pallas_call | solution.py:129
  18.2 1.7 %collective-permute-start.3 = (bf16[64,2304]{1,0:T(8,128)(2,1)S(1)}, bf16[64,2304]{1,0:T(8,128)(2,1)S(1)}, u32[]{:S(2)}, u32[]{:S(2)}) collective-permute-start(bf16[64,2304]{1,0:T(8,128)(2,1)S(1)} %shard_map.111.own_ref), channel_id=1, source_target_pairs={{0,16},{16,0},{1,17},{17,1},{2,18},{18,2},{3,19},{19,3},{4,20},{20... | collective-permute-start | bytes 884744 | tf_op jit(solution)/shard_map/ppermute | solution.py:201
  20.1 1.5 %collective-permute-done.7 = bf16[64,2176]{1,0:T(8,128)(2,1)S(1)} collective-permute-done((bf16[64,2176]{1,0:T(8,128)(2,1)S(1)}, bf16[64,2176]{1,0:T(8,128)(2,1)S(1)}, u32[]{:S(2)}, u32[]{:S(2)}) %collective-permute-start.7) | collective-permute-done | bytes 278560 | tf_op jit(solution)/shard_map/ppermute | solution.py:163
  21.6 1.7 %shard_map.112 = (bf16[64,2304]{1,0:T(8,128)(2,1)S(1)}, bf16[64,2304]{1,0:T(8,128)(2,1)S(1)}) custom-call(bf16[32,2176]{1,0:T(8,128)(2,1)S(1)} %get-tuple-element.55.refs_0_.here_ref.refs_8_, bf16[32,2176]{1,0:T(8,128)(2,1)S(1)} %get-tuple-element.50.refs_1_.there_ref.refs_9_, bf16[32,2176]{1,0:T(8,128)(2,1)S(1)} %get-tuple-element.56.refs_2_.here_ref.refs_10_, ...), custom_call_target="tpu_custom_call" | custom-call | flops 603979776 | bytes 5275648 | tf_op jit(solution)/shard_map/pallas_call | solution.py:129
  23.9 0.8 %collective-permute-start.14 = (bf16[64,2304]{1,0:T(8,128)(2,1)S(1)}, bf16[64,2304]{1,0:T(8,128)(2,1)S(1)}, u32[]{:S(2)}, u32[]{:S(2)}) collective-permute-start(bf16[64,2304]{1,0:T(8,128)(2,1)S(1)} %get-tuple-element.31.own_ref), channel_id=1, source_target_pairs={{0,16},{16,0},{1,17},{17,1},{2,18},{18,2},{3,19},{19,3},{4,20},{20... | collective-permute-start | bytes 884744 | tf_op jit(solution)/shard_map/ppermute | solution.py:201
  24.8 1.3 %collective-permute-start.17 = (bf16[64,2304]{1,0:T(8,128)(2,1)S(1)}, bf16[64,2304]{1,0:T(8,128)(2,1)S(1)}, u32[]{:S(2)}, u32[]{:S(2)}) collective-permute-start(bf16[64,2304]{1,0:T(8,128)(2,1)S(1)} %get-tuple-element.32.own_ref), channel_id=1, source_target_pairs={{0,16},{16,0},{1,17},{17,1},{2,18},{18,2},{3,19},{19,3},{4,20},{20... | collective-permute-start | bytes 884744 | tf_op jit(solution)/shard_map/ppermute | solution.py:201
  26.0 2.1 %collective-permute-done.3.other_ref = bf16[64,2304]{1,0:T(8,128)(2,1)S(1)} collective-permute-done((bf16[64,2304]{1,0:T(8,128)(2,1)S(1)}, bf16[64,2304]{1,0:T(8,128)(2,1)S(1)}, u32[]{:S(2)}, u32[]{:S(2)}) %collective-permute-start.3) | collective-permute-done | bytes 294944 | tf_op jit(solution)/shard_map/ppermute | solution.py:201
  28.2 1.0 %shard_map.113 = (bf16[64,2048]{1,0:T(8,128)(2,1)S(1)}, bf16[64,2304]{1,0:T(8,128)(2,1)S(1)}) custom-call(bf16[64,2304]{1,0:T(8,128)(2,1)S(1)} %shard_map.111.own_ref, bf16[64,2304]{1,0:T(8,128)(2,1)S(1)} %collective-permute-done.3.other_ref, bf16[32,2176]{1,0:T(8,128)(2,1)S(1)} %constant_dynamic-update-slice_fusion.refs_0_.here_ref.refs_6_, ...), custom_call_target="tpu_custom_call" | custom-call | flops 301989888 | bytes 5587456 | tf_op jit(solution)/shard_map/pallas_call | solution.py:129
  29.8 4.7 %collective-permute-done.14.other_ref = bf16[64,2304]{1,0:T(8,128)(2,1)S(1)} collective-permute-done((bf16[64,2304]{1,0:T(8,128)(2,1)S(1)}, bf16[64,2304]{1,0:T(8,128)(2,1)S(1)}, u32[]{:S(2)}, u32[]{:S(2)}) %collective-permute-start.14) | collective-permute-done | bytes 294944 | tf_op jit(solution)/shard_map/ppermute | solution.py:201
  34.5 1.0 %shard_map.115 = (bf16[64,2048]{1,0:T(8,128)(2,1)S(1)}, bf16[64,2304]{1,0:T(8,128)(2,1)S(1)}) custom-call(bf16[64,2304]{1,0:T(8,128)(2,1)S(1)} %get-tuple-element.31.own_ref, bf16[64,2304]{1,0:T(8,128)(2,1)S(1)} %collective-permute-done.14.other_ref, bf16[32,2176]{1,0:T(8,128)(2,1)S(1)} %get-tuple-element.55.refs_0_.here_ref.refs_8_, ...), custom_call_target="tpu_custom_call" | custom-call | flops 301989888 | bytes 5587456 | tf_op jit(solution)/shard_map/pallas_call | solution.py:129
  35.6 1.5 %shard_map.114.own_ref = bf16[64,2304]{1,0:T(8,128)(2,1)S(1)} custom-call(bf16[32,2176]{1,0:T(8,128)(2,1)S(1)} %constant_dynamic-update-slice_fusion.2.refs_0_.here_ref.refs_4_, bf16[32,2176]{1,0:T(8,128)(2,1)S(1)} %constant_dynamic-update-slice_fusion.4.refs_1_.there_ref.refs_5_, bf16[768,1024]{1,0:T(8,128)(2,1)S(1)} %bitcast.9, ...), custom_call_target="tpu_custom_call" | custom-call | flops 301989888 | bytes 4997120 | tf_op jit(solution)/shard_map/pallas_call | solution.py:129
  37.2 1.7 %collective-permute-start.13 = (bf16[64,2304]{1,0:T(8,128)(2,1)S(1)}, bf16[64,2304]{1,0:T(8,128)(2,1)S(1)}, u32[]{:S(2)}, u32[]{:S(2)}) collective-permute-start(bf16[64,2304]{1,0:T(8,128)(2,1)S(1)} %shard_map.114.own_ref), channel_id=1, source_target_pairs={{0,16},{16,0},{1,17},{17,1},{2,18},{18,2},{3,19},{19,3},{4,20},{20... | collective-permute-start | bytes 884744 | tf_op jit(solution)/shard_map/ppermute | solution.py:201
  38.9 1.1 %collective-permute-done.17.other_ref = bf16[64,2304]{1,0:T(8,128)(2,1)S(1)} collective-permute-done((bf16[64,2304]{1,0:T(8,128)(2,1)S(1)}, bf16[64,2304]{1,0:T(8,128)(2,1)S(1)}, u32[]{:S(2)}, u32[]{:S(2)}) %collective-permute-start.17) | collective-permute-done | bytes 294944 | tf_op jit(solution)/shard_map/ppermute | solution.py:201
  40.0 1.0 %shard_map.116 = (bf16[64,2048]{1,0:T(8,128)(2,1)S(1)}, bf16[64,2304]{1,0:T(8,128)(2,1)S(1)}) custom-call(bf16[64,2304]{1,0:T(8,128)(2,1)S(1)} %get-tuple-element.32.own_ref, bf16[64,2304]{1,0:T(8,128)(2,1)S(1)} %collective-permute-done.17.other_ref, bf16[32,2176]{1,0:T(8,128)(2,1)S(1)} %get-tuple-element.56.refs_2_.here_ref.refs_10_, ...), custom_call_target="tpu_custom_call" | custom-call | flops 301989888 | bytes 5587456 | tf_op jit(solution)/shard_map/pallas_call | solution.py:129
  41.7 1.2 %collective-permute-start.16 = (bf16[16,2048]{1,0:T(8,128)(2,1)S(1)}, bf16[16,2048]{1,0:T(8,128)(2,1)S(1)}, u32[]{:S(2)}, u32[]{:S(2)}) collective-permute-start(bf16[16,2048]{1,0:T(8,128)(2,1)S(1)} %slice.84), channel_id=1, source_target_pairs={{0,2},{1,3},{2,0},{3,1},{4,6},{5,7},{6,4},{7,5},{8,10},{9,11},{10,... | collective-permute-start | bytes 196616 | tf_op jit(solution)/shard_map/ppermute | solution.py:163
  42.9 0.9 %collective-permute-start.22 = (bf16[16,2048]{1,0:T(8,128)(2,1)S(1)}, bf16[16,2048]{1,0:T(8,128)(2,1)S(1)}, u32[]{:S(2)}, u32[]{:S(2)}) collective-permute-start(bf16[16,2048]{1,0:T(8,128)(2,1)S(1)} %slice.88), channel_id=1, source_target_pairs={{0,2},{1,3},{2,0},{3,1},{4,6},{5,7},{6,4},{7,5},{8,10},{9,11},{10,... | collective-permute-start | bytes 196616 | tf_op jit(solution)/shard_map/ppermute | solution.py:163
  43.8 2.5 %collective-permute-done.16 = bf16[16,2048]{1,0:T(8,128)(2,1)S(1)} collective-permute-done((bf16[16,2048]{1,0:T(8,128)(2,1)S(1)}, bf16[16,2048]{1,0:T(8,128)(2,1)S(1)}, u32[]{:S(2)}, u32[]{:S(2)}) %collective-permute-start.16) | collective-permute-done | bytes 65568 | tf_op jit(solution)/shard_map/ppermute | solution.py:163
  46.3 2.2 %collective-permute-start.21 = (bf16[16,2048]{1,0:T(8,128)(2,1)S(1)}, bf16[16,2048]{1,0:T(8,128)(2,1)S(1)}, u32[]{:S(2)}, u32[]{:S(2)}) collective-permute-start(bf16[16,2048]{1,0:T(8,128)(2,1)S(1)} %add_convert_fusion.4), channel_id=1, source_target_pairs={{0,8},{1,9},{2,10},{3,11},{4,12},{5,13},{6,14},{7,15},{8,0},{9,1},... | collective-permute-start | bytes 196616 | tf_op jit(solution)/shard_map/ppermute | solution.py:163
  48.6 1.0 %shard_map.117 = (bf16[64,2048]{1,0:T(8,128)(2,1)S(1)}, bf16[64,2304]{1,0:T(8,128)(2,1)S(1)}) custom-call(bf16[64,2304]{1,0:T(8,128)(2,1)S(1)} %shard_map.114.own_ref, bf16[64,2304]{1,0:T(8,128)(2,1)S(1)} %collective-permute-done.13.other_ref, bf16[32,2176]{1,0:T(8,128)(2,1)S(1)} %constant_dynamic-update-slice_fusion.2.refs_0_.here_ref.refs_4_, ...), custom_call_target="tpu_custom_call" | custom-call | flops 301989888 | bytes 5587456 | tf_op jit(solution)/shard_map/pallas_call | solution.py:129
  49.8 2.1 %collective-permute-start.23 = (bf16[16,2048]{1,0:T(8,128)(2,1)S(1)}, bf16[16,2048]{1,0:T(8,128)(2,1)S(1)}, u32[]{:S(2)}, u32[]{:S(2)}) collective-permute-start(bf16[16,2048]{1,0:T(8,128)(2,1)S(1)} %add_convert_fusion.3), channel_id=1, source_target_pairs={{0,12},{1,13},{2,14},{3,15},{4,8},{5,9},{6,10},{7,11},{8,4},{9,5},... | collective-permute-start | bytes 196616 | tf_op jit(solution)/shard_map/ppermute | solution.py:163
  52.0 1.0 %collective-permute-start.20 = (bf16[16,2048]{1,0:T(8,128)(2,1)S(1)}, bf16[16,2048]{1,0:T(8,128)(2,1)S(1)}, u32[]{:S(2)}, u32[]{:S(2)}) collective-permute-start(bf16[16,2048]{1,0:T(8,128)(2,1)S(1)} %slice.105), channel_id=1, source_target_pairs={{0,2},{1,3},{2,0},{3,1},{4,6},{5,7},{6,4},{7,5},{8,10},{9,11},{10,... | collective-permute-start | bytes 196616 | tf_op jit(solution)/shard_map/ppermute | solution.py:163
  52.9 2.6 %shard_map.118 = (bf16[1,768,1024]{2,1,0:T(8,128)(2,1)}, bf16[1,768,1024]{2,1,0:T(8,128)(2,1)}, bf16[1,768,1024]{2,1,0:T(8,128)(2,1)}) custom-call(bf16[64,2304]{1,0:T(8,128)(2,1)S(1)} %get-tuple-element.42.refs_0_, bf16[64,2304]{1,0:T(8,128)(2,1)S(1)} %get-tuple-element.43.refs_1_, bf16[64,2304]{1,0:T(8,128)(2,1)S(1)} %get-tuple-element.44.refs_2_, ...), custom_call_target="tpu_custom_call" | custom-call | flops 1207959552 | bytes 4718592 | tf_op jit(solution)/shard_map/pallas_call | solution.py:145
  55.5 0.7 %collective-permute-done.23 = bf16[16,2048]{1,0:T(8,128)(2,1)S(1)} collective-permute-done((bf16[16,2048]{1,0:T(8,128)(2,1)S(1)}, bf16[16,2048]{1,0:T(8,128)(2,1)S(1)}, u32[]{:S(2)}, u32[]{:S(2)}) %collective-permute-start.23) | collective-permute-done | bytes 65568 | tf_op jit(solution)/shard_map/ppermute | solution.py:163
  56.3 0.6 %fusion.5 = (bf16[16,1024]{1,0:T(8,128)(2,1)}, bf16[16,1024]{1,0:T(8,128)(2,1)}) fusion(bf16[16,2048]{1,0:T(8,128)(2,1)S(1)} %fusion.2), kind=kLoop, calls=%fused_computation.25 | loop fusion | bytes 131072 | tf_op jit(solution)/shard_map/slice | solution.py:262
  (58 shorter events, 2.6 us)
Async XLA Ops:
  0.6 16.0 %copy-start = (bf16[1,768,1024]{2,1,0:T(8,128)(2,1)S(1)}, bf16[1,768,1024]{2,1,0:T(8,128)(2,1)}, u32[]{:S(2)}) copy-start(bf16[1,768,1024]{2,1,0:T(8,128)(2,1)} %param.11) | copy-start | bytes 4718596
  0.7 16.0 %copy-start.1 = (bf16[1,768,1024]{2,1,0:T(8,128)(2,1)S(1)}, bf16[1,768,1024]{2,1,0:T(8,128)(2,1)}, u32[]{:S(2)}) copy-start(bf16[1,768,1024]{2,1,0:T(8,128)(2,1)} %param.12) | copy-start | bytes 4718596
  0.7 16.0 %copy-start.2 = (bf16[1,768,1024]{2,1,0:T(8,128)(2,1)S(1)}, bf16[1,768,1024]{2,1,0:T(8,128)(2,1)}, u32[]{:S(2)}) copy-start(bf16[1,768,1024]{2,1,0:T(8,128)(2,1)} %param.13) | copy-start | bytes 4718596
  1.8 8.1 %collective-permute-start.5 = (bf16[16,2176]{1,0:T(8,128)(2,1)S(1)}, bf16[16,2176]{1,0:T(8,128)(2,1)S(1)}, u32[]{:S(2)}, u32[]{:S(2)}) collective-permute-start(bf16[16,2176]{1,0:T(8,128)(2,1)S(1)} %get-tuple-element.36), channel_id=1, source_target_pairs={{0,12},{1,13},{2,14},{3,15},{4,8},{5,9},{6,10},{7,11},{8,4},{9,5},... | collective-permute-start | bytes 208904 | tf_op jit(solution)/shard_map/ppermute | solution.py:163
  6.9 6.0 %collective-permute-start.4 = (bf16[16,2176]{1,0:T(8,128)(2,1)S(1)}, bf16[16,2176]{1,0:T(8,128)(2,1)S(1)}, u32[]{:S(2)}, u32[]{:S(2)}) collective-permute-start(bf16[16,2176]{1,0:T(8,128)(2,1)S(1)} %get-tuple-element.36), channel_id=1, source_target_pairs={{0,8},{1,9},{2,10},{3,11},{4,12},{5,13},{6,14},{7,15},{8,0},{9,1},... | collective-permute-start | bytes 208904 | tf_op jit(solution)/shard_map/ppermute | solution.py:163
  6.9 17.0 %collective-permute-start.11 = (bf16[16,2176]{1,0:T(8,128)(2,1)S(1)}, bf16[16,2176]{1,0:T(8,128)(2,1)S(1)}, u32[]{:S(2)}, u32[]{:S(2)}) collective-permute-start(bf16[16,2176]{1,0:T(8,128)(2,1)S(1)} %get-tuple-element.36), channel_id=1, source_target_pairs={{0,1},{1,0},{2,3},{3,2},{4,5},{5,4},{6,7},{7,6},{8,9},{9,8},{10,11... | collective-permute-start | bytes 208904 | tf_op jit(solution)/shard_map/ppermute | solution.py:163
  6.9 8.4 %collective-permute-start.1 = (bf16[16,2176]{1,0:T(8,128)(2,1)S(1)}, bf16[16,2176]{1,0:T(8,128)(2,1)S(1)}, u32[]{:S(2)}, u32[]{:S(2)}) collective-permute-start(bf16[16,2176]{1,0:T(8,128)(2,1)S(1)} %get-tuple-element.36), channel_id=1, source_target_pairs={{0,6},{1,7},{2,4},{3,5},{4,2},{5,3},{6,0},{7,1},{8,14},{9,15},{10,... | collective-permute-start | bytes 208904 | tf_op jit(solution)/shard_map/ppermute | solution.py:163
  8.6 6.6 %collective-permute-start = (bf16[16,2176]{1,0:T(8,128)(2,1)S(1)}, bf16[16,2176]{1,0:T(8,128)(2,1)S(1)}, u32[]{:S(2)}, u32[]{:S(2)}) collective-permute-start(bf16[16,2176]{1,0:T(8,128)(2,1)S(1)} %get-tuple-element.36), channel_id=1, source_target_pairs={{0,4},{1,5},{2,6},{3,7},{4,0},{5,1},{6,2},{7,3},{8,12},{9,13},{10,... | collective-permute-start | bytes 208904 | tf_op jit(solution)/shard_map/ppermute | solution.py:163
  12.9 7.0 %collective-permute-start.6 = (bf16[32,2176]{1,0:T(8,128)(2,1)S(1)}, bf16[32,2176]{1,0:T(8,128)(2,1)S(1)}, u32[]{:S(2)}, u32[]{:S(2)}) collective-permute-start(bf16[32,2176]{1,0:T(8,128)(2,1)S(1)} %pad_maximum_fusion.1), channel_id=1, source_target_pairs={{0,2},{1,3},{2,0},{3,1},{4,6},{5,7},{6,4},{7,5},{8,10},{9,11},{10,... | collective-permute-start | bytes 417800 | tf_op jit(solution)/shard_map/ppermute | solution.py:163
  15.3 1.4 %collective-permute-start.2 = (bf16[32,2176]{1,0:T(8,128)(2,1)S(1)}, bf16[32,2176]{1,0:T(8,128)(2,1)S(1)}, u32[]{:S(2)}, u32[]{:S(2)}) collective-permute-start(bf16[32,2176]{1,0:T(8,128)(2,1)S(1)} %constant_dynamic-update-slice_fusion.refs_0_.here_ref.refs_6_), channel_id=1, source_target_pairs={{0,1},{1,0},{2,3},{3,2},{4,5},{5,4},{6,7},{7,6},{8,9},{9,8},{10,11... | collective-permute-start | bytes 417800 | tf_op jit(solution)/shard_map/ppermute | solution.py:163
  18.2 9.9 %collective-permute-start.3 = (bf16[64,2304]{1,0:T(8,128)(2,1)S(1)}, bf16[64,2304]{1,0:T(8,128)(2,1)S(1)}, u32[]{:S(2)}, u32[]{:S(2)}) collective-permute-start(bf16[64,2304]{1,0:T(8,128)(2,1)S(1)} %shard_map.111.own_ref), channel_id=1, source_target_pairs={{0,16},{16,0},{1,17},{17,1},{2,18},{18,2},{3,19},{19,3},{4,20},{20... | collective-permute-start | bytes 884744 | tf_op jit(solution)/shard_map/ppermute | solution.py:201
  20.0 1.6 %collective-permute-start.7 = (bf16[64,2176]{1,0:T(8,128)(2,1)S(1)}, bf16[64,2176]{1,0:T(8,128)(2,1)S(1)}, u32[]{:S(2)}, u32[]{:S(2)}) collective-permute-start(bf16[64,2176]{1,0:T(8,128)(2,1)S(1)} %pad_maximum_fusion), channel_id=1, source_target_pairs={{0,1},{1,0},{2,3},{3,2},{4,5},{5,4},{6,7},{7,6},{8,9},{9,8},{10,11... | collective-permute-start | bytes 835592 | tf_op jit(solution)/shard_map/ppermute | solution.py:163
  23.3 6.0 %collective-permute-start.10 = (bf16[16,2176]{1,0:T(8,128)(2,1)S(1)}, bf16[16,2176]{1,0:T(8,128)(2,1)S(1)}, u32[]{:S(2)}, u32[]{:S(2)}) collective-permute-start(bf16[16,2176]{1,0:T(8,128)(2,1)S(1)} %get-tuple-element.36), channel_id=1, source_target_pairs={{0,2},{1,3},{2,0},{3,1},{4,6},{5,7},{6,4},{7,5},{8,10},{9,11},{10,... | collective-permute-start | bytes 208904 | tf_op jit(solution)/shard_map/ppermute | solution.py:163
  23.9 10.5 %collective-permute-start.14 = (bf16[64,2304]{1,0:T(8,128)(2,1)S(1)}, bf16[64,2304]{1,0:T(8,128)(2,1)S(1)}, u32[]{:S(2)}, u32[]{:S(2)}) collective-permute-start(bf16[64,2304]{1,0:T(8,128)(2,1)S(1)} %get-tuple-element.31.own_ref), channel_id=1, source_target_pairs={{0,16},{16,0},{1,17},{17,1},{2,18},{18,2},{3,19},{19,3},{4,20},{20... | collective-permute-start | bytes 884744 | tf_op jit(solution)/shard_map/ppermute | solution.py:201
  24.8 15.2 %collective-permute-start.17 = (bf16[64,2304]{1,0:T(8,128)(2,1)S(1)}, bf16[64,2304]{1,0:T(8,128)(2,1)S(1)}, u32[]{:S(2)}, u32[]{:S(2)}) collective-permute-start(bf16[64,2304]{1,0:T(8,128)(2,1)S(1)} %get-tuple-element.32.own_ref), channel_id=1, source_target_pairs={{0,16},{16,0},{1,17},{17,1},{2,18},{18,2},{3,19},{19,3},{4,20},{20... | collective-permute-start | bytes 884744 | tf_op jit(solution)/shard_map/ppermute | solution.py:201
  29.2 11.9 %collective-permute-start.8 = (bf16[32,2048]{1,0:T(8,128)(2,1)S(1)}, bf16[32,2048]{1,0:T(8,128)(2,1)S(1)}, u32[]{:S(2)}, u32[]{:S(2)}) collective-permute-start(bf16[32,2048]{1,0:T(8,128)(2,1)S(1)} %slice.66), channel_id=1, source_target_pairs={{0,1},{1,0},{2,3},{3,2},{4,5},{5,4},{6,7},{7,6},{8,9},{9,8},{10,11... | collective-permute-start | bytes 393224 | tf_op jit(solution)/shard_map/ppermute | solution.py:163
  29.3 6.3 %collective-permute-start.12 = (bf16[16,2176]{1,0:T(8,128)(2,1)S(1)}, bf16[16,2176]{1,0:T(8,128)(2,1)S(1)}, u32[]{:S(2)}, u32[]{:S(2)}) collective-permute-start(bf16[16,2176]{1,0:T(8,128)(2,1)S(1)} %collective-permute-done.10), channel_id=1, source_target_pairs={{0,1},{1,0},{2,3},{3,2},{4,5},{5,4},{6,7},{7,6},{8,9},{9,8},{10,11... | collective-permute-start | bytes 208904 | tf_op jit(solution)/shard_map/ppermute | solution.py:163
  35.5 3.4 %collective-permute-start.15 = (bf16[32,2048]{1,0:T(8,128)(2,1)S(1)}, bf16[32,2048]{1,0:T(8,128)(2,1)S(1)}, u32[]{:S(2)}, u32[]{:S(2)}) collective-permute-start(bf16[32,2048]{1,0:T(8,128)(2,1)S(1)} %slice.68), channel_id=1, source_target_pairs={{0,1},{1,0},{2,3},{3,2},{4,5},{5,4},{6,7},{7,6},{8,9},{9,8},{10,11... | collective-permute-start | bytes 393224 | tf_op jit(solution)/shard_map/ppermute | solution.py:163
  37.2 11.4 %collective-permute-start.13 = (bf16[64,2304]{1,0:T(8,128)(2,1)S(1)}, bf16[64,2304]{1,0:T(8,128)(2,1)S(1)}, u32[]{:S(2)}, u32[]{:S(2)}) collective-permute-start(bf16[64,2304]{1,0:T(8,128)(2,1)S(1)} %shard_map.114.own_ref), channel_id=1, source_target_pairs={{0,16},{16,0},{1,17},{17,1},{2,18},{18,2},{3,19},{19,3},{4,20},{20... | collective-permute-start | bytes 884744 | tf_op jit(solution)/shard_map/ppermute | solution.py:201
  41.1 1.8 %collective-permute-start.18 = (bf16[32,2048]{1,0:T(8,128)(2,1)S(1)}, bf16[32,2048]{1,0:T(8,128)(2,1)S(1)}, u32[]{:S(2)}, u32[]{:S(2)}) collective-permute-start(bf16[32,2048]{1,0:T(8,128)(2,1)S(1)} %slice.72), channel_id=1, source_target_pairs={{0,1},{1,0},{2,3},{3,2},{4,5},{5,4},{6,7},{7,6},{8,9},{9,8},{10,11... | collective-permute-start | bytes 393224 | tf_op jit(solution)/shard_map/ppermute | solution.py:163
  41.2 10.7 %collective-permute-start.9 = (bf16[32,2048]{1,0:T(8,128)(2,1)S(1)}, bf16[32,2048]{1,0:T(8,128)(2,1)S(1)}, u32[]{:S(2)}, u32[]{:S(2)}) collective-permute-start(bf16[32,2048]{1,0:T(8,128)(2,1)S(1)} %add_convert_fusion.2), channel_id=1, source_target_pairs={{0,4},{1,5},{2,6},{3,7},{4,0},{5,1},{6,2},{7,3},{8,12},{9,13},{10,... | collective-permute-start | bytes 393224 | tf_op jit(solution)/shard_map/ppermute | solution.py:163
  41.7 4.7 %collective-permute-start.16 = (bf16[16,2048]{1,0:T(8,128)(2,1)S(1)}, bf16[16,2048]{1,0:T(8,128)(2,1)S(1)}, u32[]{:S(2)}, u32[]{:S(2)}) collective-permute-start(bf16[16,2048]{1,0:T(8,128)(2,1)S(1)} %slice.84), channel_id=1, source_target_pairs={{0,2},{1,3},{2,0},{3,1},{4,6},{5,7},{6,4},{7,5},{8,10},{9,11},{10,... | collective-permute-start | bytes 196616 | tf_op jit(solution)/shard_map/ppermute | solution.py:163
  42.9 6.8 %collective-permute-start.22 = (bf16[16,2048]{1,0:T(8,128)(2,1)S(1)}, bf16[16,2048]{1,0:T(8,128)(2,1)S(1)}, u32[]{:S(2)}, u32[]{:S(2)}) collective-permute-start(bf16[16,2048]{1,0:T(8,128)(2,1)S(1)} %slice.88), channel_id=1, source_target_pairs={{0,2},{1,3},{2,0},{3,1},{4,6},{5,7},{6,4},{7,5},{8,10},{9,11},{10,... | collective-permute-start | bytes 196616 | tf_op jit(solution)/shard_map/ppermute | solution.py:163
  46.3 9.2 %collective-permute-start.21 = (bf16[16,2048]{1,0:T(8,128)(2,1)S(1)}, bf16[16,2048]{1,0:T(8,128)(2,1)S(1)}, u32[]{:S(2)}, u32[]{:S(2)}) collective-permute-start(bf16[16,2048]{1,0:T(8,128)(2,1)S(1)} %add_convert_fusion.4), channel_id=1, source_target_pairs={{0,8},{1,9},{2,10},{3,11},{4,12},{5,13},{6,14},{7,15},{8,0},{9,1},... | collective-permute-start | bytes 196616 | tf_op jit(solution)/shard_map/ppermute | solution.py:163
  49.6 2.3 %collective-permute-start.19 = (bf16[32,2048]{1,0:T(8,128)(2,1)S(1)}, bf16[32,2048]{1,0:T(8,128)(2,1)S(1)}, u32[]{:S(2)}, u32[]{:S(2)}) collective-permute-start(bf16[32,2048]{1,0:T(8,128)(2,1)S(1)} %slice.74), channel_id=1, source_target_pairs={{0,1},{1,0},{2,3},{3,2},{4,5},{5,4},{6,7},{7,6},{8,9},{9,8},{10,11... | collective-permute-start | bytes 393224 | tf_op jit(solution)/shard_map/ppermute | solution.py:163
  49.8 6.5 %collective-permute-start.23 = (bf16[16,2048]{1,0:T(8,128)(2,1)S(1)}, bf16[16,2048]{1,0:T(8,128)(2,1)S(1)}, u32[]{:S(2)}, u32[]{:S(2)}) collective-permute-start(bf16[16,2048]{1,0:T(8,128)(2,1)S(1)} %add_convert_fusion.3), channel_id=1, source_target_pairs={{0,12},{1,13},{2,14},{3,15},{4,8},{5,9},{6,10},{7,11},{8,4},{9,5},... | collective-permute-start | bytes 196616 | tf_op jit(solution)/shard_map/ppermute | solution.py:163
  52.0 4.3 %collective-permute-start.20 = (bf16[16,2048]{1,0:T(8,128)(2,1)S(1)}, bf16[16,2048]{1,0:T(8,128)(2,1)S(1)}, u32[]{:S(2)}, u32[]{:S(2)}) collective-permute-start(bf16[16,2048]{1,0:T(8,128)(2,1)S(1)} %slice.105), channel_id=1, source_target_pairs={{0,2},{1,3},{2,0},{3,1},{4,6},{5,7},{6,4},{7,5},{8,10},{9,11},{10,... | collective-permute-start | bytes 196616 | tf_op jit(solution)/shard_map/ppermute | solution.py:163

commit v3 on v2

--- a/solution.py
+++ b/solution.py
@@ -200,12 +200,13 @@
     def other(share):
         return lax.ppermute(share, "dp", [(0, 1), (1, 0)])
 
-    def post(share, arrived, here, there):
+    def post(share, arrived, here, there, *first):
         n = share.shape[0]
+        mark = after(pick, *first) if first else pick
         return call(
             post_kernel,
             (jax.ShapeDtypeStruct((n, 2 * cols), bf16), jax.ShapeDtypeStruct((n, 3 * ff), bf16)),
-            share, arrived, here, there, pick, *weights,
+            share, arrived, here, there, mark, *weights,
             free=(4, 5, 6, 7),
             flops=6 * n * ff * cols,
         )
@@ -240,19 +241,26 @@
     (share0,) = shares_of((here0, there0), (n,))
     other0 = other(share0)
 
-    out1, act1 = post(share1, after(other1, *shares), here1, there1)
-    near = swap(fold(out1, 1).astype(bf16), 4).astype(f32)
-    acts, halves, quarters, back = [], [], [], []
-    for k, share, arrived, h, t in zip(far, shares, others, here, there):
-        out, act = post(share, after(arrived, *halves[-1:]), h, t)
-        halves.append(fold(out, 1).astype(bf16))
-        quarters.append(fold(halves[-1], 2).astype(bf16))
-        back.append(swap(quarters[-1], 4 * k))
+    out1, act1 = post(share1, other1, here1, there1, *shares)
+    near1 = swap(fold(out1, 1).astype(bf16), 4)
+    joined = [near1]
+    acts, quarters, back = [], [], []
+    for i, k in enumerate(far):
+        out, act = post(shares[i], others[i], here[i], there[i], *((near1,) if i else ()))
         acts.append(act)
-    out0, act0 = post(share0, after(other0, quarters[0], halves[-1]), here0, there0)
-    total = fold(near + fold(out0, 1), 2)
-    for b in back:
-        total += b.astype(f32)
+        half = fold(out, 1).astype(bf16)
+        if i < len(far) - 1:
+            quarters.append(fold(half, 2).astype(bf16))
+            back.append(swap(quarters[-1], 4 * k))
+        else:
+            joined.append(swap(half, 4 * k))
+    out0, act0 = post(share0, other0, here0, there0, *quarters)
+    total = joined[0].astype(f32) + fold(out0, 1)
+    for a in joined[1:]:
+        total += a.astype(f32)
+    total = fold(total, 2)
+    for a in back:
+        total += a.astype(f32)
     total = total.astype(bf16)
     gg, gu, gd = grads(
         (act0, act1, *acts),

time: 57.1 us -> 55.2 us (0.967)
  starting transfers between devices: 24.6 us -> 22.5 us
    ppermute x20 -> x19, starting transfers between devices: 19.1 us -> 17 us  [swap(): return lax.ppermute(a, 'expert', [(i, i ^ bits) for i in range(n)])]
    ppermute x20 -> x19, waiting for transfers between devices: 9.91 us -> 10.2 us  [swap(): return lax.ppermute(a, 'expert', [(i, i ^ bits) for i in range(n)])]
  transfers between devices with their start and end apart: 24 -> 23, of which waited for: 10 -> 14; matrix products, arithmetic and copies ran while one was open for 1% -> 1% of each run, Pallas kernels for 20% -> 21%
where the time goes in v3:
time: 55.2 us; the launch traced here: 55.1 us
  starting transfers between devices  22.5 us (41%)
  waiting for transfers between devices  18.1 us (33%)
  Pallas kernels  12.4 us (22%)
  between operations  0.94 us (2%)
  local copies, waits for them, and re-layouts  0.8 us (1%)
    ppermute x19, starting transfers between devices, swap(): return lax.ppermute(a, 'expert', [(i, i ^ bits) for i in range(n)])  17 us
    ppermute x19, waiting for transfers between devices, swap(): return lax.ppermute(a, 'expert', [(i, i ^ bits) for i in range(n)])  10.2 us
    pallas_call x8, Pallas kernels, call(): pl.pallas_call(kernel, out_shape=jax.tree.map(lambda o: pltpu.VMEM(o.shap...  9.84 us
    ppermute x4, waiting for transfers between devices, other(): return lax.ppermute(share, 'dp', [(0, 1), (1, 0)])  7.9 us
    ppermute x4, starting transfers between devices, other(): return lax.ppermute(share, 'dp', [(0, 1), (1, 0)])  5.49 us
    pallas_call x1, Pallas kernels, grads(): pl.pallas_call(functools.partial(grad_kernel, steps, count), out_shape=(s...  2.58 us
  transfers between devices with their start and end apart: 23, of which 14 were waited for; matrix products, arithmetic and copies ran while one was open for 1% of the time, Pallas kernels for 21%

profile of v3, /device:TPU:0, one launch (start us, length us, event | category | flops | bytes accessed | tf_op | source)
XLA Modules:
  0.0 55.1 jit_solution(18257955452784209002)
XLA Ops:
  0.7 1.1 %shard_map.110 = (bf16[16,2176]{1,0:T(8,128)(2,1)S(1)}, f32[1,128]{1,0:T(1,128)S(1)}) custom-call(bf16[16,1024]{1,0:T(8,128)(2,1)} %x_hbm.1, bf16[16,1024]{1,0:T(8,128)(2,1)} %d_hbm.1, s32[8,16]{1,0:T(8,128)} %bitcast.26, f32[8,16]{1,0:T(8,128)} %bitcast.27, f32[1,128]{1,0:T(1,128)S(1)} %and_convert_fusion.lane_ref), custom_call_target="tpu_custom_call" | custom-call | flops 30000001024 | bytes 67072 | tf_op jit(solution)/shard_map/pallas_call | solution.py:129
  1.8 5.1 %collective-permute-start.5 = (bf16[16,2176]{1,0:T(8,128)(2,1)S(1)}, bf16[16,2176]{1,0:T(8,128)(2,1)S(1)}, u32[]{:S(2)}, u32[]{:S(2)}) collective-permute-start(bf16[16,2176]{1,0:T(8,128)(2,1)S(1)} %get-tuple-element.36), channel_id=1, source_target_pairs={{0,12},{1,13},{2,14},{3,15},{4,8},{5,9},{6,10},{7,11},{8,4},{9,5},... | collective-permute-start | bytes 208904 | tf_op jit(solution)/shard_map/ppermute | solution.py:163
  6.9 1.7 %collective-permute-start.1 = (bf16[16,2176]{1,0:T(8,128)(2,1)S(1)}, bf16[16,2176]{1,0:T(8,128)(2,1)S(1)}, u32[]{:S(2)}, u32[]{:S(2)}) collective-permute-start(bf16[16,2176]{1,0:T(8,128)(2,1)S(1)} %get-tuple-element.36), channel_id=1, source_target_pairs={{0,6},{1,7},{2,4},{3,5},{4,2},{5,3},{6,0},{7,1},{8,14},{9,15},{10,... | collective-permute-start | bytes 208904 | tf_op jit(solution)/shard_map/ppermute | solution.py:163
  8.6 1.2 %collective-permute-start = (bf16[16,2176]{1,0:T(8,128)(2,1)S(1)}, bf16[16,2176]{1,0:T(8,128)(2,1)S(1)}, u32[]{:S(2)}, u32[]{:S(2)}) collective-permute-start(bf16[16,2176]{1,0:T(8,128)(2,1)S(1)} %get-tuple-element.36), channel_id=1, source_target_pairs={{0,4},{1,5},{2,6},{3,7},{4,0},{5,1},{6,2},{7,3},{8,12},{9,13},{10,... | collective-permute-start | bytes 208904 | tf_op jit(solution)/shard_map/ppermute | solution.py:163
  9.9 3.0 %collective-permute-done.4 = bf16[16,2176]{1,0:T(8,128)(2,1)S(1)} collective-permute-done((bf16[16,2176]{1,0:T(8,128)(2,1)S(1)}, bf16[16,2176]{1,0:T(8,128)(2,1)S(1)}, u32[]{:S(2)}, u32[]{:S(2)}) %collective-permute-start.4) | collective-permute-done | bytes 69664 | tf_op jit(solution)/shard_map/ppermute | solution.py:163
  12.9 1.6 %collective-permute-start.6 = (bf16[32,2176]{1,0:T(8,128)(2,1)S(1)}, bf16[32,2176]{1,0:T(8,128)(2,1)S(1)}, u32[]{:S(2)}, u32[]{:S(2)}) collective-permute-start(bf16[32,2176]{1,0:T(8,128)(2,1)S(1)} %pad_maximum_fusion.1), channel_id=1, source_target_pairs={{0,2},{1,3},{2,0},{3,1},{4,6},{5,7},{6,4},{7,5},{8,10},{9,11},{10,... | collective-permute-start | bytes 417800 | tf_op jit(solution)/shard_map/ppermute | solution.py:163
  14.5 0.7 %collective-permute-done = bf16[16,2176]{1,0:T(8,128)(2,1)S(1)} collective-permute-done((bf16[16,2176]{1,0:T(8,128)(2,1)S(1)}, bf16[16,2176]{1,0:T(8,128)(2,1)S(1)}, u32[]{:S(2)}, u32[]{:S(2)}) %collective-permute-start) | collective-permute-done | bytes 69664 | tf_op jit(solution)/shard_map/ppermute | solution.py:163
  15.4 1.3 %collective-permute-done.2.refs_1_.there_ref.refs_7_ = bf16[32,2176]{1,0:T(8,128)(2,1)S(1)} collective-permute-done((bf16[32,2176]{1,0:T(8,128)(2,1)S(1)}, bf16[32,2176]{1,0:T(8,128)(2,1)S(1)}, u32[]{:S(2)}, u32[]{:S(2)}) %collective-permute-start.2) | collective-permute-done | bytes 139296 | tf_op jit(solution)/shard_map/ppermute | solution.py:163
  16.7 1.5 %shard_map.111.own_ref = bf16[64,2304]{1,0:T(8,128)(2,1)S(1)} custom-call(bf16[32,2176]{1,0:T(8,128)(2,1)S(1)} %constant_dynamic-update-slice_fusion.refs_0_.here_ref.refs_6_, bf16[32,2176]{1,0:T(8,128)(2,1)S(1)} %collective-permute-done.2.refs_1_.there_ref.refs_7_, bf16[768,1024]{1,0:T(8,128)(2,1)S(1)} %bitcast.5, bf16[768,1024]{1,0:T(8,128)(2,1)S(1)} %bitcast.12, ...), custom_call_target="tpu_custom_call" | custom-call | flops 301989888 | bytes 4997120 | tf_op jit(solution)/shard_map/pallas_call | solution.py:129
  18.2 1.7 %collective-permute-start.3 = (bf16[64,2304]{1,0:T(8,128)(2,1)S(1)}, bf16[64,2304]{1,0:T(8,128)(2,1)S(1)}, u32[]{:S(2)}, u32[]{:S(2)}) collective-permute-start(bf16[64,2304]{1,0:T(8,128)(2,1)S(1)} %shard_map.111.own_ref), channel_id=1, source_target_pairs={{0,16},{16,0},{1,17},{17,1},{2,18},{18,2},{3,19},{19,3},{4,20},{20... | collective-permute-start | bytes 884744 | tf_op jit(solution)/shard_map/ppermute | solution.py:201
  20.1 1.5 %collective-permute-done.7 = bf16[64,2176]{1,0:T(8,128)(2,1)S(1)} collective-permute-done((bf16[64,2176]{1,0:T(8,128)(2,1)S(1)}, bf16[64,2176]{1,0:T(8,128)(2,1)S(1)}, u32[]{:S(2)}, u32[]{:S(2)}) %collective-permute-start.7) | collective-permute-done | bytes 278560 | tf_op jit(solution)/shard_map/ppermute | solution.py:163
  21.6 1.6 %shard_map.112 = (bf16[64,2304]{1,0:T(8,128)(2,1)S(1)}, bf16[64,2304]{1,0:T(8,128)(2,1)S(1)}) custom-call(bf16[32,2176]{1,0:T(8,128)(2,1)S(1)} %get-tuple-element.55.refs_0_.here_ref.refs_8_, bf16[32,2176]{1,0:T(8,128)(2,1)S(1)} %get-tuple-element.50.refs_1_.there_ref.refs_9_, bf16[32,2176]{1,0:T(8,128)(2,1)S(1)} %get-tuple-element.56.refs_2_.here_ref.refs_10_, ...), custom_call_target="tpu_custom_call" | custom-call | flops 603979776 | bytes 5275648 | tf_op jit(solution)/shard_map/pallas_call | solution.py:129
  23.9 0.8 %collective-permute-start.14 = (bf16[64,2304]{1,0:T(8,128)(2,1)S(1)}, bf16[64,2304]{1,0:T(8,128)(2,1)S(1)}, u32[]{:S(2)}, u32[]{:S(2)}) collective-permute-start(bf16[64,2304]{1,0:T(8,128)(2,1)S(1)} %get-tuple-element.32.own_ref), channel_id=1, source_target_pairs={{0,16},{16,0},{1,17},{17,1},{2,18},{18,2},{3,19},{19,3},{4,20},{20... | collective-permute-start | bytes 884744 | tf_op jit(solution)/shard_map/ppermute | solution.py:201
  24.8 1.3 %collective-permute-start.18 = (bf16[64,2304]{1,0:T(8,128)(2,1)S(1)}, bf16[64,2304]{1,0:T(8,128)(2,1)S(1)}, u32[]{:S(2)}, u32[]{:S(2)}) collective-permute-start(bf16[64,2304]{1,0:T(8,128)(2,1)S(1)} %get-tuple-element.33.own_ref), channel_id=1, source_target_pairs={{0,16},{16,0},{1,17},{17,1},{2,18},{18,2},{3,19},{19,3},{4,20},{20... | collective-permute-start | bytes 884744 | tf_op jit(solution)/shard_map/ppermute | solution.py:201
  26.0 2.2 %collective-permute-done.3.other_ref = bf16[64,2304]{1,0:T(8,128)(2,1)S(1)} collective-permute-done((bf16[64,2304]{1,0:T(8,128)(2,1)S(1)}, bf16[64,2304]{1,0:T(8,128)(2,1)S(1)}, u32[]{:S(2)}, u32[]{:S(2)}) %collective-permute-start.3) | collective-permute-done | bytes 294944 | tf_op jit(solution)/shard_map/ppermute | solution.py:201
  28.2 1.0 %shard_map.113 = (bf16[64,2048]{1,0:T(8,128)(2,1)S(1)}, bf16[64,2304]{1,0:T(8,128)(2,1)S(1)}) custom-call(bf16[64,2304]{1,0:T(8,128)(2,1)S(1)} %shard_map.111.own_ref, bf16[64,2304]{1,0:T(8,128)(2,1)S(1)} %collective-permute-done.3.other_ref, bf16[32,2176]{1,0:T(8,128)(2,1)S(1)} %constant_dynamic-update-slice_fusion.refs_0_.here_ref.refs_6_, ...), custom_call_target="tpu_custom_call" | custom-call | flops 301989888 | bytes 5587456 | tf_op jit(solution)/shard_map/pallas_call | solution.py:129
  29.8 0.8 %collective-permute-done.8 = bf16[32,2048]{1,0:T(8,128)(2,1)S(1)} collective-permute-done((bf16[32,2048]{1,0:T(8,128)(2,1)S(1)}, bf16[32,2048]{1,0:T(8,128)(2,1)S(1)}, u32[]{:S(2)}, u32[]{:S(2)}) %collective-permute-start.8) | collective-permute-done | bytes 131104 | tf_op jit(solution)/shard_map/ppermute | solution.py:163
  30.7 3.7 %collective-permute-done.14.other_ref = bf16[64,2304]{1,0:T(8,128)(2,1)S(1)} collective-permute-done((bf16[64,2304]{1,0:T(8,128)(2,1)S(1)}, bf16[64,2304]{1,0:T(8,128)(2,1)S(1)}, u32[]{:S(2)}, u32[]{:S(2)}) %collective-permute-start.14) | collective-permute-done | bytes 294944 | tf_op jit(solution)/shard_map/ppermute | solution.py:201
  34.5 1.0 %shard_map.115 = (bf16[64,2048]{1,0:T(8,128)(2,1)S(1)}, bf16[64,2304]{1,0:T(8,128)(2,1)S(1)}) custom-call(bf16[64,2304]{1,0:T(8,128)(2,1)S(1)} %get-tuple-element.32.own_ref, bf16[64,2304]{1,0:T(8,128)(2,1)S(1)} %collective-permute-done.14.other_ref, bf16[32,2176]{1,0:T(8,128)(2,1)S(1)} %get-tuple-element.55.refs_0_.here_ref.refs_8_, ...), custom_call_target="tpu_custom_call" | custom-call | flops 301989888 | bytes 5587456 | tf_op jit(solution)/shard_map/pallas_call | solution.py:129
  35.6 1.5 %shard_map.114.own_ref = bf16[64,2304]{1,0:T(8,128)(2,1)S(1)} custom-call(bf16[32,2176]{1,0:T(8,128)(2,1)S(1)} %constant_dynamic-update-slice_fusion.2.refs_0_.here_ref.refs_4_, bf16[32,2176]{1,0:T(8,128)(2,1)S(1)} %constant_dynamic-update-slice_fusion.4.refs_1_.there_ref.refs_5_, bf16[768,1024]{1,0:T(8,128)(2,1)S(1)} %bitcast.9, ...), custom_call_target="tpu_custom_call" | custom-call | flops 301989888 | bytes 4997120 | tf_op jit(solution)/shard_map/pallas_call | solution.py:129
  37.2 1.7 %collective-permute-start.13 = (bf16[64,2304]{1,0:T(8,128)(2,1)S(1)}, bf16[64,2304]{1,0:T(8,128)(2,1)S(1)}, u32[]{:S(2)}, u32[]{:S(2)}) collective-permute-start(bf16[64,2304]{1,0:T(8,128)(2,1)S(1)} %shard_map.114.own_ref), channel_id=1, source_target_pairs={{0,16},{16,0},{1,17},{17,1},{2,18},{18,2},{3,19},{19,3},{4,20},{20... | collective-permute-start | bytes 884744 | tf_op jit(solution)/shard_map/ppermute | solution.py:201
  38.9 1.1 %collective-permute-done.18.other_ref = bf16[64,2304]{1,0:T(8,128)(2,1)S(1)} collective-permute-done((bf16[64,2304]{1,0:T(8,128)(2,1)S(1)}, bf16[64,2304]{1,0:T(8,128)(2,1)S(1)}, u32[]{:S(2)}, u32[]{:S(2)}) %collective-permute-start.18) | collective-permute-done | bytes 294944 | tf_op jit(solution)/shard_map/ppermute | solution.py:201
  40.0 1.0 %shard_map.117 = (bf16[64,2048]{1,0:T(8,128)(2,1)S(1)}, bf16[64,2304]{1,0:T(8,128)(2,1)S(1)}) custom-call(bf16[64,2304]{1,0:T(8,128)(2,1)S(1)} %get-tuple-element.33.own_ref, bf16[64,2304]{1,0:T(8,128)(2,1)S(1)} %collective-permute-done.18.other_ref, bf16[32,2176]{1,0:T(8,128)(2,1)S(1)} %get-tuple-element.56.refs_2_.here_ref.refs_10_, ...), custom_call_target="tpu_custom_call" | custom-call | flops 301989888 | bytes 5587456 | tf_op jit(solution)/shard_map/pallas_call | solution.py:129
  41.2 0.8 %collective-permute-start.16 = (bf16[16,2048]{1,0:T(8,128)(2,1)S(1)}, bf16[16,2048]{1,0:T(8,128)(2,1)S(1)}, u32[]{:S(2)}, u32[]{:S(2)}) collective-permute-start(bf16[16,2048]{1,0:T(8,128)(2,1)S(1)} %slice.76), channel_id=1, source_target_pairs={{0,2},{1,3},{2,0},{3,1},{4,6},{5,7},{6,4},{7,5},{8,10},{9,11},{10,... | collective-permute-start | bytes 196616 | tf_op jit(solution)/shard_map/ppermute | solution.py:163
  42.5 2.4 %collective-permute-start.20 = (bf16[32,2048]{1,0:T(8,128)(2,1)S(1)}, bf16[32,2048]{1,0:T(8,128)(2,1)S(1)}, u32[]{:S(2)}, u32[]{:S(2)}) collective-permute-start(bf16[32,2048]{1,0:T(8,128)(2,1)S(1)} %add_convert_fusion), channel_id=1, source_target_pairs={{0,12},{1,13},{2,14},{3,15},{4,8},{5,9},{6,10},{7,11},{8,4},{9,5},... | collective-permute-start | bytes 393224 | tf_op jit(solution)/shard_map/ppermute | solution.py:163
  44.9 0.9 %collective-permute-done.16 = bf16[16,2048]{1,0:T(8,128)(2,1)S(1)} collective-permute-done((bf16[16,2048]{1,0:T(8,128)(2,1)S(1)}, bf16[16,2048]{1,0:T(8,128)(2,1)S(1)}, u32[]{:S(2)}, u32[]{:S(2)}) %collective-permute-start.16) | collective-permute-done | bytes 65568 | tf_op jit(solution)/shard_map/ppermute | solution.py:163
  45.8 0.9 %collective-permute-done.13.other_ref = bf16[64,2304]{1,0:T(8,128)(2,1)S(1)} collective-permute-done((bf16[64,2304]{1,0:T(8,128)(2,1)S(1)}, bf16[64,2304]{1,0:T(8,128)(2,1)S(1)}, u32[]{:S(2)}, u32[]{:S(2)}) %collective-permute-start.13) | collective-permute-done | bytes 294944 | tf_op jit(solution)/shard_map/ppermute | solution.py:201
  46.6 1.0 %shard_map.116 = (bf16[64,2048]{1,0:T(8,128)(2,1)S(1)}, bf16[64,2304]{1,0:T(8,128)(2,1)S(1)}) custom-call(bf16[64,2304]{1,0:T(8,128)(2,1)S(1)} %shard_map.114.own_ref, bf16[64,2304]{1,0:T(8,128)(2,1)S(1)} %collective-permute-done.13.other_ref, bf16[32,2176]{1,0:T(8,128)(2,1)S(1)} %constant_dynamic-update-slice_fusion.2.refs_0_.here_ref.refs_4_, ...), custom_call_target="tpu_custom_call" | custom-call | flops 301989888 | bytes 5587456 | tf_op jit(solution)/shard_map/pallas_call | solution.py:129
  47.7 1.7 %collective-permute-start.22 = (bf16[16,2048]{1,0:T(8,128)(2,1)S(1)}, bf16[16,2048]{1,0:T(8,128)(2,1)S(1)}, u32[]{:S(2)}, u32[]{:S(2)}) collective-permute-start(bf16[16,2048]{1,0:T(8,128)(2,1)S(1)} %add_convert_fusion.3), channel_id=1, source_target_pairs={{0,8},{1,9},{2,10},{3,11},{4,12},{5,13},{6,14},{7,15},{8,0},{9,1},... | collective-permute-start | bytes 196616 | tf_op jit(solution)/shard_map/ppermute | solution.py:163
  50.1 0.9 %collective-permute-start.21 = (bf16[16,2048]{1,0:T(8,128)(2,1)S(1)}, bf16[16,2048]{1,0:T(8,128)(2,1)S(1)}, u32[]{:S(2)}, u32[]{:S(2)}) collective-permute-start(bf16[16,2048]{1,0:T(8,128)(2,1)S(1)} %slice.92), channel_id=1, source_target_pairs={{0,2},{1,3},{2,0},{3,1},{4,6},{5,7},{6,4},{7,5},{8,10},{9,11},{10,... | collective-permute-start | bytes 196616 | tf_op jit(solution)/shard_map/ppermute | solution.py:163
  51.1 2.6 %shard_map.118 = (bf16[1,768,1024]{2,1,0:T(8,128)(2,1)}, bf16[1,768,1024]{2,1,0:T(8,128)(2,1)}, bf16[1,768,1024]{2,1,0:T(8,128)(2,1)}) custom-call(bf16[64,2304]{1,0:T(8,128)(2,1)S(1)} %get-tuple-element.42.refs_0_, bf16[64,2304]{1,0:T(8,128)(2,1)S(1)} %get-tuple-element.43.refs_1_, bf16[64,2304]{1,0:T(8,128)(2,1)S(1)} %get-tuple-element.44.refs_2_, ...), custom_call_target="tpu_custom_call" | custom-call | flops 1207959552 | bytes 4718592 | tf_op jit(solution)/shard_map/pallas_call | solution.py:145
  53.6 0.7 %collective-permute-done.22 = bf16[16,2048]{1,0:T(8,128)(2,1)S(1)} collective-permute-done((bf16[16,2048]{1,0:T(8,128)(2,1)S(1)}, bf16[16,2048]{1,0:T(8,128)(2,1)S(1)}, u32[]{:S(2)}, u32[]{:S(2)}) %collective-permute-start.22) | collective-permute-done | bytes 65568 | tf_op jit(solution)/shard_map/ppermute | solution.py:163
  (54 shorter events, 3.9 us)
Async XLA Ops:
  0.6 16.0 %copy-start = (bf16[1,768,1024]{2,1,0:T(8,128)(2,1)S(1)}, bf16[1,768,1024]{2,1,0:T(8,128)(2,1)}, u32[]{:S(2)}) copy-start(bf16[1,768,1024]{2,1,0:T(8,128)(2,1)} %param.11) | copy-start | bytes 4718596
  0.7 16.0 %copy-start.1 = (bf16[1,768,1024]{2,1,0:T(8,128)(2,1)S(1)}, bf16[1,768,1024]{2,1,0:T(8,128)(2,1)}, u32[]{:S(2)}) copy-start(bf16[1,768,1024]{2,1,0:T(8,128)(2,1)} %param.12) | copy-start | bytes 4718596
  0.7 16.0 %copy-start.2 = (bf16[1,768,1024]{2,1,0:T(8,128)(2,1)S(1)}, bf16[1,768,1024]{2,1,0:T(8,128)(2,1)}, u32[]{:S(2)}) copy-start(bf16[1,768,1024]{2,1,0:T(8,128)(2,1)} %param.13) | copy-start | bytes 4718596
  1.8 8.1 %collective-permute-start.5 = (bf16[16,2176]{1,0:T(8,128)(2,1)S(1)}, bf16[16,2176]{1,0:T(8,128)(2,1)S(1)}, u32[]{:S(2)}, u32[]{:S(2)}) collective-permute-start(bf16[16,2176]{1,0:T(8,128)(2,1)S(1)} %get-tuple-element.36), channel_id=1, source_target_pairs={{0,12},{1,13},{2,14},{3,15},{4,8},{5,9},{6,10},{7,11},{8,4},{9,5},... | collective-permute-start | bytes 208904 | tf_op jit(solution)/shard_map/ppermute | solution.py:163
  6.9 6.0 %collective-permute-start.4 = (bf16[16,2176]{1,0:T(8,128)(2,1)S(1)}, bf16[16,2176]{1,0:T(8,128)(2,1)S(1)}, u32[]{:S(2)}, u32[]{:S(2)}) collective-permute-start(bf16[16,2176]{1,0:T(8,128)(2,1)S(1)} %get-tuple-element.36), channel_id=1, source_target_pairs={{0,8},{1,9},{2,10},{3,11},{4,12},{5,13},{6,14},{7,15},{8,0},{9,1},... | collective-permute-start | bytes 208904 | tf_op jit(solution)/shard_map/ppermute | solution.py:163
  6.9 17.0 %collective-permute-start.11 = (bf16[16,2176]{1,0:T(8,128)(2,1)S(1)}, bf16[16,2176]{1,0:T(8,128)(2,1)S(1)}, u32[]{:S(2)}, u32[]{:S(2)}) collective-permute-start(bf16[16,2176]{1,0:T(8,128)(2,1)S(1)} %get-tuple-element.36), channel_id=1, source_target_pairs={{0,1},{1,0},{2,3},{3,2},{4,5},{5,4},{6,7},{7,6},{8,9},{9,8},{10,11... | collective-permute-start | bytes 208904 | tf_op jit(solution)/shard_map/ppermute | solution.py:163
  6.9 8.4 %collective-permute-start.1 = (bf16[16,2176]{1,0:T(8,128)(2,1)S(1)}, bf16[16,2176]{1,0:T(8,128)(2,1)S(1)}, u32[]{:S(2)}, u32[]{:S(2)}) collective-permute-start(bf16[16,2176]{1,0:T(8,128)(2,1)S(1)} %get-tuple-element.36), channel_id=1, source_target_pairs={{0,6},{1,7},{2,4},{3,5},{4,2},{5,3},{6,0},{7,1},{8,14},{9,15},{10,... | collective-permute-start | bytes 208904 | tf_op jit(solution)/shard_map/ppermute | solution.py:163
  8.6 6.6 %collective-permute-start = (bf16[16,2176]{1,0:T(8,128)(2,1)S(1)}, bf16[16,2176]{1,0:T(8,128)(2,1)S(1)}, u32[]{:S(2)}, u32[]{:S(2)}) collective-permute-start(bf16[16,2176]{1,0:T(8,128)(2,1)S(1)} %get-tuple-element.36), channel_id=1, source_target_pairs={{0,4},{1,5},{2,6},{3,7},{4,0},{5,1},{6,2},{7,3},{8,12},{9,13},{10,... | collective-permute-start | bytes 208904 | tf_op jit(solution)/shard_map/ppermute | solution.py:163
  12.9 7.0 %collective-permute-start.6 = (bf16[32,2176]{1,0:T(8,128)(2,1)S(1)}, bf16[32,2176]{1,0:T(8,128)(2,1)S(1)}, u32[]{:S(2)}, u32[]{:S(2)}) collective-permute-start(bf16[32,2176]{1,0:T(8,128)(2,1)S(1)} %pad_maximum_fusion.1), channel_id=1, source_target_pairs={{0,2},{1,3},{2,0},{3,1},{4,6},{5,7},{6,4},{7,5},{8,10},{9,11},{10,... | collective-permute-start | bytes 417800 | tf_op jit(solution)/shard_map/ppermute | solution.py:163
  15.3 1.4 %collective-permute-start.2 = (bf16[32,2176]{1,0:T(8,128)(2,1)S(1)}, bf16[32,2176]{1,0:T(8,128)(2,1)S(1)}, u32[]{:S(2)}, u32[]{:S(2)}) collective-permute-start(bf16[32,2176]{1,0:T(8,128)(2,1)S(1)} %constant_dynamic-update-slice_fusion.refs_0_.here_ref.refs_6_), channel_id=1, source_target_pairs={{0,1},{1,0},{2,3},{3,2},{4,5},{5,4},{6,7},{7,6},{8,9},{9,8},{10,11... | collective-permute-start | bytes 417800 | tf_op jit(solution)/shard_map/ppermute | solution.py:163
  18.2 9.9 %collective-permute-start.3 = (bf16[64,2304]{1,0:T(8,128)(2,1)S(1)}, bf16[64,2304]{1,0:T(8,128)(2,1)S(1)}, u32[]{:S(2)}, u32[]{:S(2)}) collective-permute-start(bf16[64,2304]{1,0:T(8,128)(2,1)S(1)} %shard_map.111.own_ref), channel_id=1, source_target_pairs={{0,16},{16,0},{1,17},{17,1},{2,18},{18,2},{3,19},{19,3},{4,20},{20... | collective-permute-start | bytes 884744 | tf_op jit(solution)/shard_map/ppermute | solution.py:201
  20.0 1.6 %collective-permute-start.7 = (bf16[64,2176]{1,0:T(8,128)(2,1)S(1)}, bf16[64,2176]{1,0:T(8,128)(2,1)S(1)}, u32[]{:S(2)}, u32[]{:S(2)}) collective-permute-start(bf16[64,2176]{1,0:T(8,128)(2,1)S(1)} %pad_maximum_fusion), channel_id=1, source_target_pairs={{0,1},{1,0},{2,3},{3,2},{4,5},{5,4},{6,7},{7,6},{8,9},{9,8},{10,11... | collective-permute-start | bytes 835592 | tf_op jit(solution)/shard_map/ppermute | solution.py:163
  23.3 6.0 %collective-permute-start.10 = (bf16[16,2176]{1,0:T(8,128)(2,1)S(1)}, bf16[16,2176]{1,0:T(8,128)(2,1)S(1)}, u32[]{:S(2)}, u32[]{:S(2)}) collective-permute-start(bf16[16,2176]{1,0:T(8,128)(2,1)S(1)} %get-tuple-element.36), channel_id=1, source_target_pairs={{0,2},{1,3},{2,0},{3,1},{4,6},{5,7},{6,4},{7,5},{8,10},{9,11},{10,... | collective-permute-start | bytes 208904 | tf_op jit(solution)/shard_map/ppermute | solution.py:163
  23.9 10.6 %collective-permute-start.14 = (bf16[64,2304]{1,0:T(8,128)(2,1)S(1)}, bf16[64,2304]{1,0:T(8,128)(2,1)S(1)}, u32[]{:S(2)}, u32[]{:S(2)}) collective-permute-start(bf16[64,2304]{1,0:T(8,128)(2,1)S(1)} %get-tuple-element.32.own_ref), channel_id=1, source_target_pairs={{0,16},{16,0},{1,17},{17,1},{2,18},{18,2},{3,19},{19,3},{4,20},{20... | collective-permute-start | bytes 884744 | tf_op jit(solution)/shard_map/ppermute | solution.py:201
  24.8 15.2 %collective-permute-start.18 = (bf16[64,2304]{1,0:T(8,128)(2,1)S(1)}, bf16[64,2304]{1,0:T(8,128)(2,1)S(1)}, u32[]{:S(2)}, u32[]{:S(2)}) collective-permute-start(bf16[64,2304]{1,0:T(8,128)(2,1)S(1)} %get-tuple-element.33.own_ref), channel_id=1, source_target_pairs={{0,16},{16,0},{1,17},{17,1},{2,18},{18,2},{3,19},{19,3},{4,20},{20... | collective-permute-start | bytes 884744 | tf_op jit(solution)/shard_map/ppermute | solution.py:201
  29.2 1.4 %collective-permute-start.8 = (bf16[32,2048]{1,0:T(8,128)(2,1)S(1)}, bf16[32,2048]{1,0:T(8,128)(2,1)S(1)}, u32[]{:S(2)}, u32[]{:S(2)}) collective-permute-start(bf16[32,2048]{1,0:T(8,128)(2,1)S(1)} %slice.60), channel_id=1, source_target_pairs={{0,1},{1,0},{2,3},{3,2},{4,5},{5,4},{6,7},{7,6},{8,9},{9,8},{10,11... | collective-permute-start | bytes 393224 | tf_op jit(solution)/shard_map/ppermute | solution.py:163
  29.3 6.3 %collective-permute-start.12 = (bf16[16,2176]{1,0:T(8,128)(2,1)S(1)}, bf16[16,2176]{1,0:T(8,128)(2,1)S(1)}, u32[]{:S(2)}, u32[]{:S(2)}) collective-permute-start(bf16[16,2176]{1,0:T(8,128)(2,1)S(1)} %collective-permute-done.10), channel_id=1, source_target_pairs={{0,1},{1,0},{2,3},{3,2},{4,5},{5,4},{6,7},{7,6},{8,9},{9,8},{10,11... | collective-permute-start | bytes 208904 | tf_op jit(solution)/shard_map/ppermute | solution.py:163
  30.7 8.2 %collective-permute-start.9 = (bf16[32,2048]{1,0:T(8,128)(2,1)S(1)}, bf16[32,2048]{1,0:T(8,128)(2,1)S(1)}, u32[]{:S(2)}, u32[]{:S(2)}) collective-permute-start(bf16[32,2048]{1,0:T(8,128)(2,1)S(1)} %add_convert_fusion.2), channel_id=1, source_target_pairs={{0,4},{1,5},{2,6},{3,7},{4,0},{5,1},{6,2},{7,3},{8,12},{9,13},{10,... | collective-permute-start | bytes 393224 | tf_op jit(solution)/shard_map/ppermute | solution.py:163
  35.5 5.6 %collective-permute-start.15 = (bf16[32,2048]{1,0:T(8,128)(2,1)S(1)}, bf16[32,2048]{1,0:T(8,128)(2,1)S(1)}, u32[]{:S(2)}, u32[]{:S(2)}) collective-permute-start(bf16[32,2048]{1,0:T(8,128)(2,1)S(1)} %slice.62), channel_id=1, source_target_pairs={{0,1},{1,0},{2,3},{3,2},{4,5},{5,4},{6,7},{7,6},{8,9},{9,8},{10,11... | collective-permute-start | bytes 393224 | tf_op jit(solution)/shard_map/ppermute | solution.py:163
  37.2 9.5 %collective-permute-start.13 = (bf16[64,2304]{1,0:T(8,128)(2,1)S(1)}, bf16[64,2304]{1,0:T(8,128)(2,1)S(1)}, u32[]{:S(2)}, u32[]{:S(2)}) collective-permute-start(bf16[64,2304]{1,0:T(8,128)(2,1)S(1)} %shard_map.114.own_ref), channel_id=1, source_target_pairs={{0,16},{16,0},{1,17},{17,1},{2,18},{18,2},{3,19},{19,3},{4,20},{20... | collective-permute-start | bytes 884744 | tf_op jit(solution)/shard_map/ppermute | solution.py:201
  41.0 1.4 %collective-permute-start.19 = (bf16[32,2048]{1,0:T(8,128)(2,1)S(1)}, bf16[32,2048]{1,0:T(8,128)(2,1)S(1)}, u32[]{:S(2)}, u32[]{:S(2)}) collective-permute-start(bf16[32,2048]{1,0:T(8,128)(2,1)S(1)} %slice.68), channel_id=1, source_target_pairs={{0,1},{1,0},{2,3},{3,2},{4,5},{5,4},{6,7},{7,6},{8,9},{9,8},{10,11... | collective-permute-start | bytes 393224 | tf_op jit(solution)/shard_map/ppermute | solution.py:163
  41.2 4.5 %collective-permute-start.16 = (bf16[16,2048]{1,0:T(8,128)(2,1)S(1)}, bf16[16,2048]{1,0:T(8,128)(2,1)S(1)}, u32[]{:S(2)}, u32[]{:S(2)}) collective-permute-start(bf16[16,2048]{1,0:T(8,128)(2,1)S(1)} %slice.76), channel_id=1, source_target_pairs={{0,2},{1,3},{2,0},{3,1},{4,6},{5,7},{6,4},{7,5},{8,10},{9,11},{10,... | collective-permute-start | bytes 196616 | tf_op jit(solution)/shard_map/ppermute | solution.py:163
  42.5 7.5 %collective-permute-start.20 = (bf16[32,2048]{1,0:T(8,128)(2,1)S(1)}, bf16[32,2048]{1,0:T(8,128)(2,1)S(1)}, u32[]{:S(2)}, u32[]{:S(2)}) collective-permute-start(bf16[32,2048]{1,0:T(8,128)(2,1)S(1)} %add_convert_fusion), channel_id=1, source_target_pairs={{0,12},{1,13},{2,14},{3,15},{4,8},{5,9},{6,10},{7,11},{8,4},{9,5},... | collective-permute-start | bytes 393224 | tf_op jit(solution)/shard_map/ppermute | solution.py:163
  47.7 2.4 %collective-permute-start.17 = (bf16[32,2048]{1,0:T(8,128)(2,1)S(1)}, bf16[32,2048]{1,0:T(8,128)(2,1)S(1)}, u32[]{:S(2)}, u32[]{:S(2)}) collective-permute-start(bf16[32,2048]{1,0:T(8,128)(2,1)S(1)} %slice.66), channel_id=1, source_target_pairs={{0,1},{1,0},{2,3},{3,2},{4,5},{5,4},{6,7},{7,6},{8,9},{9,8},{10,11... | collective-permute-start | bytes 393224 | tf_op jit(solution)/shard_map/ppermute | solution.py:163
  47.7 6.6 %collective-permute-start.22 = (bf16[16,2048]{1,0:T(8,128)(2,1)S(1)}, bf16[16,2048]{1,0:T(8,128)(2,1)S(1)}, u32[]{:S(2)}, u32[]{:S(2)}) collective-permute-start(bf16[16,2048]{1,0:T(8,128)(2,1)S(1)} %add_convert_fusion.3), channel_id=1, source_target_pairs={{0,8},{1,9},{2,10},{3,11},{4,12},{5,13},{6,14},{7,15},{8,0},{9,1},... | collective-permute-start | bytes 196616 | tf_op jit(solution)/shard_map/ppermute | solution.py:163
  50.1 4.3 %collective-permute-start.21 = (bf16[16,2048]{1,0:T(8,128)(2,1)S(1)}, bf16[16,2048]{1,0:T(8,128)(2,1)S(1)}, u32[]{:S(2)}, u32[]{:S(2)}) collective-permute-start(bf16[16,2048]{1,0:T(8,128)(2,1)S(1)} %slice.92), channel_id=1, source_target_pairs={{0,2},{1,3},{2,0},{3,1},{4,6},{5,7},{6,4},{7,5},{8,10},{9,11},{10,... | collective-permute-start | bytes 196616 | tf_op jit(solution)/shard_map/ppermute | solution.py:163

commit v4 on v3

--- a/solution.py
+++ b/solution.py
@@ -246,7 +246,7 @@
     joined = [near1]
     acts, quarters, back = [], [], []
     for i, k in enumerate(far):
-        out, act = post(shares[i], others[i], here[i], there[i], *((near1,) if i else ()))
+        out, act = post(shares[i], others[i], here[i], there[i], *((near1, share0) if i else ()))
         acts.append(act)
         half = fold(out, 1).astype(bf16)
         if i < len(far) - 1:

time: 55.2 us -> 55.2 us (level)
  no operation moved by 1% of the time
where the time goes in v4:
time: 55.2 us; the launch traced here: 55.1 us
  starting transfers between devices  22.5 us (41%)
  waiting for transfers between devices  18.1 us (33%)
  Pallas kernels  12.4 us (22%)
  between operations  0.94 us (2%)
  local copies, waits for them, and re-layouts  0.8 us (1%)
    ppermute x19, starting transfers between devices, swap(): return lax.ppermute(a, 'expert', [(i, i ^ bits) for i in range(n)])  17 us
    ppermute x19, waiting for transfers between devices, swap(): return lax.ppermute(a, 'expert', [(i, i ^ bits) for i in range(n)])  10.2 us
    pallas_call x8, Pallas kernels, call(): pl.pallas_call(kernel, out_shape=jax.tree.map(lambda o: pltpu.VMEM(o.shap...  9.84 us
    ppermute x4, waiting for transfers between devices, other(): return lax.ppermute(share, 'dp', [(0, 1), (1, 0)])  7.9 us
    ppermute x4, starting transfers between devices, other(): return lax.ppermute(share, 'dp', [(0, 1), (1, 0)])  5.49 us
    pallas_call x1, Pallas kernels, grads(): pl.pallas_call(functools.partial(grad_kernel, steps, count), out_shape=(s...  2.58 us
  transfers between devices with their start and end apart: 23, of which 14 were waited for; matrix products, arithmetic and copies ran while one was open for 1% of the time, Pallas kernels for 21%

profile of v4, /device:TPU:0, one launch (start us, length us, event | category | flops | bytes accessed | tf_op | source)
XLA Modules:
  0.0 55.1 jit_solution(18257955452784209002)
XLA Ops:
  0.7 1.1 %shard_map.110 = (bf16[16,2176]{1,0:T(8,128)(2,1)S(1)}, f32[1,128]{1,0:T(1,128)S(1)}) custom-call(bf16[16,1024]{1,0:T(8,128)(2,1)} %x_hbm.1, bf16[16,1024]{1,0:T(8,128)(2,1)} %d_hbm.1, s32[8,16]{1,0:T(8,128)} %bitcast.26, f32[8,16]{1,0:T(8,128)} %bitcast.27, f32[1,128]{1,0:T(1,128)S(1)} %and_convert_fusion.lane_ref), custom_call_target="tpu_custom_call" | custom-call | flops 30000001024 | bytes 67072 | tf_op jit(solution)/shard_map/pallas_call | solution.py:129
  1.8 5.1 %collective-permute-start.5 = (bf16[16,2176]{1,0:T(8,128)(2,1)S(1)}, bf16[16,2176]{1,0:T(8,128)(2,1)S(1)}, u32[]{:S(2)}, u32[]{:S(2)}) collective-permute-start(bf16[16,2176]{1,0:T(8,128)(2,1)S(1)} %get-tuple-element.36), channel_id=1, source_target_pairs={{0,12},{1,13},{2,14},{3,15},{4,8},{5,9},{6,10},{7,11},{8,4},{9,5},... | collective-permute-start | bytes 208904 | tf_op jit(solution)/shard_map/ppermute | solution.py:163
  6.9 1.7 %collective-permute-start.1 = (bf16[16,2176]{1,0:T(8,128)(2,1)S(1)}, bf16[16,2176]{1,0:T(8,128)(2,1)S(1)}, u32[]{:S(2)}, u32[]{:S(2)}) collective-permute-start(bf16[16,2176]{1,0:T(8,128)(2,1)S(1)} %get-tuple-element.36), channel_id=1, source_target_pairs={{0,6},{1,7},{2,4},{3,5},{4,2},{5,3},{6,0},{7,1},{8,14},{9,15},{10,... | collective-permute-start | bytes 208904 | tf_op jit(solution)/shard_map/ppermute | solution.py:163
  8.6 1.2 %collective-permute-start = (bf16[16,2176]{1,0:T(8,128)(2,1)S(1)}, bf16[16,2176]{1,0:T(8,128)(2,1)S(1)}, u32[]{:S(2)}, u32[]{:S(2)}) collective-permute-start(bf16[16,2176]{1,0:T(8,128)(2,1)S(1)} %get-tuple-element.36), channel_id=1, source_target_pairs={{0,4},{1,5},{2,6},{3,7},{4,0},{5,1},{6,2},{7,3},{8,12},{9,13},{10,... | collective-permute-start | bytes 208904 | tf_op jit(solution)/shard_map/ppermute | solution.py:163
  9.9 3.0 %collective-permute-done.4 = bf16[16,2176]{1,0:T(8,128)(2,1)S(1)} collective-permute-done((bf16[16,2176]{1,0:T(8,128)(2,1)S(1)}, bf16[16,2176]{1,0:T(8,128)(2,1)S(1)}, u32[]{:S(2)}, u32[]{:S(2)}) %collective-permute-start.4) | collective-permute-done | bytes 69664 | tf_op jit(solution)/shard_map/ppermute | solution.py:163
  12.9 1.6 %collective-permute-start.6 = (bf16[32,2176]{1,0:T(8,128)(2,1)S(1)}, bf16[32,2176]{1,0:T(8,128)(2,1)S(1)}, u32[]{:S(2)}, u32[]{:S(2)}) collective-permute-start(bf16[32,2176]{1,0:T(8,128)(2,1)S(1)} %pad_maximum_fusion.1), channel_id=1, source_target_pairs={{0,2},{1,3},{2,0},{3,1},{4,6},{5,7},{6,4},{7,5},{8,10},{9,11},{10,... | collective-permute-start | bytes 417800 | tf_op jit(solution)/shard_map/ppermute | solution.py:163
  14.5 0.7 %collective-permute-done = bf16[16,2176]{1,0:T(8,128)(2,1)S(1)} collective-permute-done((bf16[16,2176]{1,0:T(8,128)(2,1)S(1)}, bf16[16,2176]{1,0:T(8,128)(2,1)S(1)}, u32[]{:S(2)}, u32[]{:S(2)}) %collective-permute-start) | collective-permute-done | bytes 69664 | tf_op jit(solution)/shard_map/ppermute | solution.py:163
  15.4 1.3 %collective-permute-done.2.refs_1_.there_ref.refs_7_ = bf16[32,2176]{1,0:T(8,128)(2,1)S(1)} collective-permute-done((bf16[32,2176]{1,0:T(8,128)(2,1)S(1)}, bf16[32,2176]{1,0:T(8,128)(2,1)S(1)}, u32[]{:S(2)}, u32[]{:S(2)}) %collective-permute-start.2) | collective-permute-done | bytes 139296 | tf_op jit(solution)/shard_map/ppermute | solution.py:163
  16.7 1.5 %shard_map.111.own_ref = bf16[64,2304]{1,0:T(8,128)(2,1)S(1)} custom-call(bf16[32,2176]{1,0:T(8,128)(2,1)S(1)} %constant_dynamic-update-slice_fusion.refs_0_.here_ref.refs_6_, bf16[32,2176]{1,0:T(8,128)(2,1)S(1)} %collective-permute-done.2.refs_1_.there_ref.refs_7_, bf16[768,1024]{1,0:T(8,128)(2,1)S(1)} %bitcast.5, bf16[768,1024]{1,0:T(8,128)(2,1)S(1)} %bitcast.12, ...), custom_call_target="tpu_custom_call" | custom-call | flops 301989888 | bytes 4997120 | tf_op jit(solution)/shard_map/pallas_call | solution.py:129
  18.2 1.7 %collective-permute-start.3 = (bf16[64,2304]{1,0:T(8,128)(2,1)S(1)}, bf16[64,2304]{1,0:T(8,128)(2,1)S(1)}, u32[]{:S(2)}, u32[]{:S(2)}) collective-permute-start(bf16[64,2304]{1,0:T(8,128)(2,1)S(1)} %shard_map.111.own_ref), channel_id=1, source_target_pairs={{0,16},{16,0},{1,17},{17,1},{2,18},{18,2},{3,19},{19,3},{4,20},{20... | collective-permute-start | bytes 884744 | tf_op jit(solution)/shard_map/ppermute | solution.py:201
  20.1 1.5 %collective-permute-done.7 = bf16[64,2176]{1,0:T(8,128)(2,1)S(1)} collective-permute-done((bf16[64,2176]{1,0:T(8,128)(2,1)S(1)}, bf16[64,2176]{1,0:T(8,128)(2,1)S(1)}, u32[]{:S(2)}, u32[]{:S(2)}) %collective-permute-start.7) | collective-permute-done | bytes 278560 | tf_op jit(solution)/shard_map/ppermute | solution.py:163
  21.6 1.6 %shard_map.112 = (bf16[64,2304]{1,0:T(8,128)(2,1)S(1)}, bf16[64,2304]{1,0:T(8,128)(2,1)S(1)}) custom-call(bf16[32,2176]{1,0:T(8,128)(2,1)S(1)} %get-tuple-element.55.refs_0_.here_ref.refs_8_, bf16[32,2176]{1,0:T(8,128)(2,1)S(1)} %get-tuple-element.50.refs_1_.there_ref.refs_9_, bf16[32,2176]{1,0:T(8,128)(2,1)S(1)} %get-tuple-element.56.refs_2_.here_ref.refs_10_, ...), custom_call_target="tpu_custom_call" | custom-call | flops 603979776 | bytes 5275648 | tf_op jit(solution)/shard_map/pallas_call | solution.py:129
  23.9 0.8 %collective-permute-start.14 = (bf16[64,2304]{1,0:T(8,128)(2,1)S(1)}, bf16[64,2304]{1,0:T(8,128)(2,1)S(1)}, u32[]{:S(2)}, u32[]{:S(2)}) collective-permute-start(bf16[64,2304]{1,0:T(8,128)(2,1)S(1)} %get-tuple-element.32.own_ref), channel_id=1, source_target_pairs={{0,16},{16,0},{1,17},{17,1},{2,18},{18,2},{3,19},{19,3},{4,20},{20... | collective-permute-start | bytes 884744 | tf_op jit(solution)/shard_map/ppermute | solution.py:201
  24.8 1.3 %collective-permute-start.18 = (bf16[64,2304]{1,0:T(8,128)(2,1)S(1)}, bf16[64,2304]{1,0:T(8,128)(2,1)S(1)}, u32[]{:S(2)}, u32[]{:S(2)}) collective-permute-start(bf16[64,2304]{1,0:T(8,128)(2,1)S(1)} %get-tuple-element.33.own_ref), channel_id=1, source_target_pairs={{0,16},{16,0},{1,17},{17,1},{2,18},{18,2},{3,19},{19,3},{4,20},{20... | collective-permute-start | bytes 884744 | tf_op jit(solution)/shard_map/ppermute | solution.py:201
  26.0 2.2 %collective-permute-done.3.other_ref = bf16[64,2304]{1,0:T(8,128)(2,1)S(1)} collective-permute-done((bf16[64,2304]{1,0:T(8,128)(2,1)S(1)}, bf16[64,2304]{1,0:T(8,128)(2,1)S(1)}, u32[]{:S(2)}, u32[]{:S(2)}) %collective-permute-start.3) | collective-permute-done | bytes 294944 | tf_op jit(solution)/shard_map/ppermute | solution.py:201
  28.2 1.0 %shard_map.113 = (bf16[64,2048]{1,0:T(8,128)(2,1)S(1)}, bf16[64,2304]{1,0:T(8,128)(2,1)S(1)}) custom-call(bf16[64,2304]{1,0:T(8,128)(2,1)S(1)} %shard_map.111.own_ref, bf16[64,2304]{1,0:T(8,128)(2,1)S(1)} %collective-permute-done.3.other_ref, bf16[32,2176]{1,0:T(8,128)(2,1)S(1)} %constant_dynamic-update-slice_fusion.refs_0_.here_ref.refs_6_, ...), custom_call_target="tpu_custom_call" | custom-call | flops 301989888 | bytes 5587456 | tf_op jit(solution)/shard_map/pallas_call | solution.py:129
  29.8 0.8 %collective-permute-done.8 = bf16[32,2048]{1,0:T(8,128)(2,1)S(1)} collective-permute-done((bf16[32,2048]{1,0:T(8,128)(2,1)S(1)}, bf16[32,2048]{1,0:T(8,128)(2,1)S(1)}, u32[]{:S(2)}, u32[]{:S(2)}) %collective-permute-start.8) | collective-permute-done | bytes 131104 | tf_op jit(solution)/shard_map/ppermute | solution.py:163
  30.7 3.7 %collective-permute-done.14.other_ref = bf16[64,2304]{1,0:T(8,128)(2,1)S(1)} collective-permute-done((bf16[64,2304]{1,0:T(8,128)(2,1)S(1)}, bf16[64,2304]{1,0:T(8,128)(2,1)S(1)}, u32[]{:S(2)}, u32[]{:S(2)}) %collective-permute-start.14) | collective-permute-done | bytes 294944 | tf_op jit(solution)/shard_map/ppermute | solution.py:201
  34.5 1.0 %shard_map.115 = (bf16[64,2048]{1,0:T(8,128)(2,1)S(1)}, bf16[64,2304]{1,0:T(8,128)(2,1)S(1)}) custom-call(bf16[64,2304]{1,0:T(8,128)(2,1)S(1)} %get-tuple-element.32.own_ref, bf16[64,2304]{1,0:T(8,128)(2,1)S(1)} %collective-permute-done.14.other_ref, bf16[32,2176]{1,0:T(8,128)(2,1)S(1)} %get-tuple-element.55.refs_0_.here_ref.refs_8_, ...), custom_call_target="tpu_custom_call" | custom-call | flops 301989888 | bytes 5587456 | tf_op jit(solution)/shard_map/pallas_call | solution.py:129
  35.6 1.5 %shard_map.114.own_ref = bf16[64,2304]{1,0:T(8,128)(2,1)S(1)} custom-call(bf16[32,2176]{1,0:T(8,128)(2,1)S(1)} %constant_dynamic-update-slice_fusion.2.refs_0_.here_ref.refs_4_, bf16[32,2176]{1,0:T(8,128)(2,1)S(1)} %constant_dynamic-update-slice_fusion.4.refs_1_.there_ref.refs_5_, bf16[768,1024]{1,0:T(8,128)(2,1)S(1)} %bitcast.9, ...), custom_call_target="tpu_custom_call" | custom-call | flops 301989888 | bytes 4997120 | tf_op jit(solution)/shard_map/pallas_call | solution.py:129
  37.2 1.7 %collective-permute-start.13 = (bf16[64,2304]{1,0:T(8,128)(2,1)S(1)}, bf16[64,2304]{1,0:T(8,128)(2,1)S(1)}, u32[]{:S(2)}, u32[]{:S(2)}) collective-permute-start(bf16[64,2304]{1,0:T(8,128)(2,1)S(1)} %shard_map.114.own_ref), channel_id=1, source_target_pairs={{0,16},{16,0},{1,17},{17,1},{2,18},{18,2},{3,19},{19,3},{4,20},{20... | collective-permute-start | bytes 884744 | tf_op jit(solution)/shard_map/ppermute | solution.py:201
  38.9 1.1 %collective-permute-done.18.other_ref = bf16[64,2304]{1,0:T(8,128)(2,1)S(1)} collective-permute-done((bf16[64,2304]{1,0:T(8,128)(2,1)S(1)}, bf16[64,2304]{1,0:T(8,128)(2,1)S(1)}, u32[]{:S(2)}, u32[]{:S(2)}) %collective-permute-start.18) | collective-permute-done | bytes 294944 | tf_op jit(solution)/shard_map/ppermute | solution.py:201
  40.0 1.0 %shard_map.117 = (bf16[64,2048]{1,0:T(8,128)(2,1)S(1)}, bf16[64,2304]{1,0:T(8,128)(2,1)S(1)}) custom-call(bf16[64,2304]{1,0:T(8,128)(2,1)S(1)} %get-tuple-element.33.own_ref, bf16[64,2304]{1,0:T(8,128)(2,1)S(1)} %collective-permute-done.18.other_ref, bf16[32,2176]{1,0:T(8,128)(2,1)S(1)} %get-tuple-element.56.refs_2_.here_ref.refs_10_, ...), custom_call_target="tpu_custom_call" | custom-call | flops 301989888 | bytes 5587456 | tf_op jit(solution)/shard_map/pallas_call | solution.py:129
  41.2 0.8 %collective-permute-start.16 = (bf16[16,2048]{1,0:T(8,128)(2,1)S(1)}, bf16[16,2048]{1,0:T(8,128)(2,1)S(1)}, u32[]{:S(2)}, u32[]{:S(2)}) collective-permute-start(bf16[16,2048]{1,0:T(8,128)(2,1)S(1)} %slice.76), channel_id=1, source_target_pairs={{0,2},{1,3},{2,0},{3,1},{4,6},{5,7},{6,4},{7,5},{8,10},{9,11},{10,... | collective-permute-start | bytes 196616 | tf_op jit(solution)/shard_map/ppermute | solution.py:163
  42.5 2.4 %collective-permute-start.20 = (bf16[32,2048]{1,0:T(8,128)(2,1)S(1)}, bf16[32,2048]{1,0:T(8,128)(2,1)S(1)}, u32[]{:S(2)}, u32[]{:S(2)}) collective-permute-start(bf16[32,2048]{1,0:T(8,128)(2,1)S(1)} %add_convert_fusion), channel_id=1, source_target_pairs={{0,12},{1,13},{2,14},{3,15},{4,8},{5,9},{6,10},{7,11},{8,4},{9,5},... | collective-permute-start | bytes 393224 | tf_op jit(solution)/shard_map/ppermute | solution.py:163
  44.9 0.9 %collective-permute-done.16 = bf16[16,2048]{1,0:T(8,128)(2,1)S(1)} collective-permute-done((bf16[16,2048]{1,0:T(8,128)(2,1)S(1)}, bf16[16,2048]{1,0:T(8,128)(2,1)S(1)}, u32[]{:S(2)}, u32[]{:S(2)}) %collective-permute-start.16) | collective-permute-done | bytes 65568 | tf_op jit(solution)/shard_map/ppermute | solution.py:163
  45.8 0.9 %collective-permute-done.13.other_ref = bf16[64,2304]{1,0:T(8,128)(2,1)S(1)} collective-permute-done((bf16[64,2304]{1,0:T(8,128)(2,1)S(1)}, bf16[64,2304]{1,0:T(8,128)(2,1)S(1)}, u32[]{:S(2)}, u32[]{:S(2)}) %collective-permute-start.13) | collective-permute-done | bytes 294944 | tf_op jit(solution)/shard_map/ppermute | solution.py:201
  46.6 1.0 %shard_map.116 = (bf16[64,2048]{1,0:T(8,128)(2,1)S(1)}, bf16[64,2304]{1,0:T(8,128)(2,1)S(1)}) custom-call(bf16[64,2304]{1,0:T(8,128)(2,1)S(1)} %shard_map.114.own_ref, bf16[64,2304]{1,0:T(8,128)(2,1)S(1)} %collective-permute-done.13.other_ref, bf16[32,2176]{1,0:T(8,128)(2,1)S(1)} %constant_dynamic-update-slice_fusion.2.refs_0_.here_ref.refs_4_, ...), custom_call_target="tpu_custom_call" | custom-call | flops 301989888 | bytes 5587456 | tf_op jit(solution)/shard_map/pallas_call | solution.py:129
  47.7 1.7 %collective-permute-start.22 = (bf16[16,2048]{1,0:T(8,128)(2,1)S(1)}, bf16[16,2048]{1,0:T(8,128)(2,1)S(1)}, u32[]{:S(2)}, u32[]{:S(2)}) collective-permute-start(bf16[16,2048]{1,0:T(8,128)(2,1)S(1)} %add_convert_fusion.3), channel_id=1, source_target_pairs={{0,8},{1,9},{2,10},{3,11},{4,12},{5,13},{6,14},{7,15},{8,0},{9,1},... | collective-permute-start | bytes 196616 | tf_op jit(solution)/shard_map/ppermute | solution.py:163
  50.1 0.9 %collective-permute-start.21 = (bf16[16,2048]{1,0:T(8,128)(2,1)S(1)}, bf16[16,2048]{1,0:T(8,128)(2,1)S(1)}, u32[]{:S(2)}, u32[]{:S(2)}) collective-permute-start(bf16[16,2048]{1,0:T(8,128)(2,1)S(1)} %slice.92), channel_id=1, source_target_pairs={{0,2},{1,3},{2,0},{3,1},{4,6},{5,7},{6,4},{7,5},{8,10},{9,11},{10,... | collective-permute-start | bytes 196616 | tf_op jit(solution)/shard_map/ppermute | solution.py:163
  51.1 2.6 %shard_map.118 = (bf16[1,768,1024]{2,1,0:T(8,128)(2,1)}, bf16[1,768,1024]{2,1,0:T(8,128)(2,1)}, bf16[1,768,1024]{2,1,0:T(8,128)(2,1)}) custom-call(bf16[64,2304]{1,0:T(8,128)(2,1)S(1)} %get-tuple-element.42.refs_0_, bf16[64,2304]{1,0:T(8,128)(2,1)S(1)} %get-tuple-element.43.refs_1_, bf16[64,2304]{1,0:T(8,128)(2,1)S(1)} %get-tuple-element.44.refs_2_, ...), custom_call_target="tpu_custom_call" | custom-call | flops 1207959552 | bytes 4718592 | tf_op jit(solution)/shard_map/pallas_call | solution.py:145
  53.6 0.7 %collective-permute-done.22 = bf16[16,2048]{1,0:T(8,128)(2,1)S(1)} collective-permute-done((bf16[16,2048]{1,0:T(8,128)(2,1)S(1)}, bf16[16,2048]{1,0:T(8,128)(2,1)S(1)}, u32[]{:S(2)}, u32[]{:S(2)}) %collective-permute-start.22) | collective-permute-done | bytes 65568 | tf_op jit(solution)/shard_map/ppermute | solution.py:163
  (54 shorter events, 3.9 us)
Async XLA Ops:
  0.6 16.0 %copy-start = (bf16[1,768,1024]{2,1,0:T(8,128)(2,1)S(1)}, bf16[1,768,1024]{2,1,0:T(8,128)(2,1)}, u32[]{:S(2)}) copy-start(bf16[1,768,1024]{2,1,0:T(8,128)(2,1)} %param.11) | copy-start | bytes 4718596
  0.7 16.0 %copy-start.1 = (bf16[1,768,1024]{2,1,0:T(8,128)(2,1)S(1)}, bf16[1,768,1024]{2,1,0:T(8,128)(2,1)}, u32[]{:S(2)}) copy-start(bf16[1,768,1024]{2,1,0:T(8,128)(2,1)} %param.12) | copy-start | bytes 4718596
  0.7 16.0 %copy-start.2 = (bf16[1,768,1024]{2,1,0:T(8,128)(2,1)S(1)}, bf16[1,768,1024]{2,1,0:T(8,128)(2,1)}, u32[]{:S(2)}) copy-start(bf16[1,768,1024]{2,1,0:T(8,128)(2,1)} %param.13) | copy-start | bytes 4718596
  1.8 8.1 %collective-permute-start.5 = (bf16[16,2176]{1,0:T(8,128)(2,1)S(1)}, bf16[16,2176]{1,0:T(8,128)(2,1)S(1)}, u32[]{:S(2)}, u32[]{:S(2)}) collective-permute-start(bf16[16,2176]{1,0:T(8,128)(2,1)S(1)} %get-tuple-element.36), channel_id=1, source_target_pairs={{0,12},{1,13},{2,14},{3,15},{4,8},{5,9},{6,10},{7,11},{8,4},{9,5},... | collective-permute-start | bytes 208904 | tf_op jit(solution)/shard_map/ppermute | solution.py:163
  6.9 6.0 %collective-permute-start.4 = (bf16[16,2176]{1,0:T(8,128)(2,1)S(1)}, bf16[16,2176]{1,0:T(8,128)(2,1)S(1)}, u32[]{:S(2)}, u32[]{:S(2)}) collective-permute-start(bf16[16,2176]{1,0:T(8,128)(2,1)S(1)} %get-tuple-element.36), channel_id=1, source_target_pairs={{0,8},{1,9},{2,10},{3,11},{4,12},{5,13},{6,14},{7,15},{8,0},{9,1},... | collective-permute-start | bytes 208904 | tf_op jit(solution)/shard_map/ppermute | solution.py:163
  6.9 17.0 %collective-permute-start.11 = (bf16[16,2176]{1,0:T(8,128)(2,1)S(1)}, bf16[16,2176]{1,0:T(8,128)(2,1)S(1)}, u32[]{:S(2)}, u32[]{:S(2)}) collective-permute-start(bf16[16,2176]{1,0:T(8,128)(2,1)S(1)} %get-tuple-element.36), channel_id=1, source_target_pairs={{0,1},{1,0},{2,3},{3,2},{4,5},{5,4},{6,7},{7,6},{8,9},{9,8},{10,11... | collective-permute-start | bytes 208904 | tf_op jit(solution)/shard_map/ppermute | solution.py:163
  6.9 8.4 %collective-permute-start.1 = (bf16[16,2176]{1,0:T(8,128)(2,1)S(1)}, bf16[16,2176]{1,0:T(8,128)(2,1)S(1)}, u32[]{:S(2)}, u32[]{:S(2)}) collective-permute-start(bf16[16,2176]{1,0:T(8,128)(2,1)S(1)} %get-tuple-element.36), channel_id=1, source_target_pairs={{0,6},{1,7},{2,4},{3,5},{4,2},{5,3},{6,0},{7,1},{8,14},{9,15},{10,... | collective-permute-start | bytes 208904 | tf_op jit(solution)/shard_map/ppermute | solution.py:163
  8.6 6.6 %collective-permute-start = (bf16[16,2176]{1,0:T(8,128)(2,1)S(1)}, bf16[16,2176]{1,0:T(8,128)(2,1)S(1)}, u32[]{:S(2)}, u32[]{:S(2)}) collective-permute-start(bf16[16,2176]{1,0:T(8,128)(2,1)S(1)} %get-tuple-element.36), channel_id=1, source_target_pairs={{0,4},{1,5},{2,6},{3,7},{4,0},{5,1},{6,2},{7,3},{8,12},{9,13},{10,... | collective-permute-start | bytes 208904 | tf_op jit(solution)/shard_map/ppermute | solution.py:163
  12.9 7.0 %collective-permute-start.6 = (bf16[32,2176]{1,0:T(8,128)(2,1)S(1)}, bf16[32,2176]{1,0:T(8,128)(2,1)S(1)}, u32[]{:S(2)}, u32[]{:S(2)}) collective-permute-start(bf16[32,2176]{1,0:T(8,128)(2,1)S(1)} %pad_maximum_fusion.1), channel_id=1, source_target_pairs={{0,2},{1,3},{2,0},{3,1},{4,6},{5,7},{6,4},{7,5},{8,10},{9,11},{10,... | collective-permute-start | bytes 417800 | tf_op jit(solution)/shard_map/ppermute | solution.py:163
  15.3 1.4 %collective-permute-start.2 = (bf16[32,2176]{1,0:T(8,128)(2,1)S(1)}, bf16[32,2176]{1,0:T(8,128)(2,1)S(1)}, u32[]{:S(2)}, u32[]{:S(2)}) collective-permute-start(bf16[32,2176]{1,0:T(8,128)(2,1)S(1)} %constant_dynamic-update-slice_fusion.refs_0_.here_ref.refs_6_), channel_id=1, source_target_pairs={{0,1},{1,0},{2,3},{3,2},{4,5},{5,4},{6,7},{7,6},{8,9},{9,8},{10,11... | collective-permute-start | bytes 417800 | tf_op jit(solution)/shard_map/ppermute | solution.py:163
  18.2 9.9 %collective-permute-start.3 = (bf16[64,2304]{1,0:T(8,128)(2,1)S(1)}, bf16[64,2304]{1,0:T(8,128)(2,1)S(1)}, u32[]{:S(2)}, u32[]{:S(2)}) collective-permute-start(bf16[64,2304]{1,0:T(8,128)(2,1)S(1)} %shard_map.111.own_ref), channel_id=1, source_target_pairs={{0,16},{16,0},{1,17},{17,1},{2,18},{18,2},{3,19},{19,3},{4,20},{20... | collective-permute-start | bytes 884744 | tf_op jit(solution)/shard_map/ppermute | solution.py:201
  20.0 1.6 %collective-permute-start.7 = (bf16[64,2176]{1,0:T(8,128)(2,1)S(1)}, bf16[64,2176]{1,0:T(8,128)(2,1)S(1)}, u32[]{:S(2)}, u32[]{:S(2)}) collective-permute-start(bf16[64,2176]{1,0:T(8,128)(2,1)S(1)} %pad_maximum_fusion), channel_id=1, source_target_pairs={{0,1},{1,0},{2,3},{3,2},{4,5},{5,4},{6,7},{7,6},{8,9},{9,8},{10,11... | collective-permute-start | bytes 835592 | tf_op jit(solution)/shard_map/ppermute | solution.py:163
  23.3 6.0 %collective-permute-start.10 = (bf16[16,2176]{1,0:T(8,128)(2,1)S(1)}, bf16[16,2176]{1,0:T(8,128)(2,1)S(1)}, u32[]{:S(2)}, u32[]{:S(2)}) collective-permute-start(bf16[16,2176]{1,0:T(8,128)(2,1)S(1)} %get-tuple-element.36), channel_id=1, source_target_pairs={{0,2},{1,3},{2,0},{3,1},{4,6},{5,7},{6,4},{7,5},{8,10},{9,11},{10,... | collective-permute-start | bytes 208904 | tf_op jit(solution)/shard_map/ppermute | solution.py:163
  23.9 10.6 %collective-permute-start.14 = (bf16[64,2304]{1,0:T(8,128)(2,1)S(1)}, bf16[64,2304]{1,0:T(8,128)(2,1)S(1)}, u32[]{:S(2)}, u32[]{:S(2)}) collective-permute-start(bf16[64,2304]{1,0:T(8,128)(2,1)S(1)} %get-tuple-element.32.own_ref), channel_id=1, source_target_pairs={{0,16},{16,0},{1,17},{17,1},{2,18},{18,2},{3,19},{19,3},{4,20},{20... | collective-permute-start | bytes 884744 | tf_op jit(solution)/shard_map/ppermute | solution.py:201
  24.8 15.2 %collective-permute-start.18 = (bf16[64,2304]{1,0:T(8,128)(2,1)S(1)}, bf16[64,2304]{1,0:T(8,128)(2,1)S(1)}, u32[]{:S(2)}, u32[]{:S(2)}) collective-permute-start(bf16[64,2304]{1,0:T(8,128)(2,1)S(1)} %get-tuple-element.33.own_ref), channel_id=1, source_target_pairs={{0,16},{16,0},{1,17},{17,1},{2,18},{18,2},{3,19},{19,3},{4,20},{20... | collective-permute-start | bytes 884744 | tf_op jit(solution)/shard_map/ppermute | solution.py:201
  29.2 1.4 %collective-permute-start.8 = (bf16[32,2048]{1,0:T(8,128)(2,1)S(1)}, bf16[32,2048]{1,0:T(8,128)(2,1)S(1)}, u32[]{:S(2)}, u32[]{:S(2)}) collective-permute-start(bf16[32,2048]{1,0:T(8,128)(2,1)S(1)} %slice.60), channel_id=1, source_target_pairs={{0,1},{1,0},{2,3},{3,2},{4,5},{5,4},{6,7},{7,6},{8,9},{9,8},{10,11... | collective-permute-start | bytes 393224 | tf_op jit(solution)/shard_map/ppermute | solution.py:163
  29.3 6.3 %collective-permute-start.12 = (bf16[16,2176]{1,0:T(8,128)(2,1)S(1)}, bf16[16,2176]{1,0:T(8,128)(2,1)S(1)}, u32[]{:S(2)}, u32[]{:S(2)}) collective-permute-start(bf16[16,2176]{1,0:T(8,128)(2,1)S(1)} %collective-permute-done.10), channel_id=1, source_target_pairs={{0,1},{1,0},{2,3},{3,2},{4,5},{5,4},{6,7},{7,6},{8,9},{9,8},{10,11... | collective-permute-start | bytes 208904 | tf_op jit(solution)/shard_map/ppermute | solution.py:163
  30.7 8.2 %collective-permute-start.9 = (bf16[32,2048]{1,0:T(8,128)(2,1)S(1)}, bf16[32,2048]{1,0:T(8,128)(2,1)S(1)}, u32[]{:S(2)}, u32[]{:S(2)}) collective-permute-start(bf16[32,2048]{1,0:T(8,128)(2,1)S(1)} %add_convert_fusion.2), channel_id=1, source_target_pairs={{0,4},{1,5},{2,6},{3,7},{4,0},{5,1},{6,2},{7,3},{8,12},{9,13},{10,... | collective-permute-start | bytes 393224 | tf_op jit(solution)/shard_map/ppermute | solution.py:163
  35.5 5.6 %collective-permute-start.15 = (bf16[32,2048]{1,0:T(8,128)(2,1)S(1)}, bf16[32,2048]{1,0:T(8,128)(2,1)S(1)}, u32[]{:S(2)}, u32[]{:S(2)}) collective-permute-start(bf16[32,2048]{1,0:T(8,128)(2,1)S(1)} %slice.62), channel_id=1, source_target_pairs={{0,1},{1,0},{2,3},{3,2},{4,5},{5,4},{6,7},{7,6},{8,9},{9,8},{10,11... | collective-permute-start | bytes 393224 | tf_op jit(solution)/shard_map/ppermute | solution.py:163
  37.2 9.5 %collective-permute-start.13 = (bf16[64,2304]{1,0:T(8,128)(2,1)S(1)}, bf16[64,2304]{1,0:T(8,128)(2,1)S(1)}, u32[]{:S(2)}, u32[]{:S(2)}) collective-permute-start(bf16[64,2304]{1,0:T(8,128)(2,1)S(1)} %shard_map.114.own_ref), channel_id=1, source_target_pairs={{0,16},{16,0},{1,17},{17,1},{2,18},{18,2},{3,19},{19,3},{4,20},{20... | collective-permute-start | bytes 884744 | tf_op jit(solution)/shard_map/ppermute | solution.py:201
  41.0 1.4 %collective-permute-start.19 = (bf16[32,2048]{1,0:T(8,128)(2,1)S(1)}, bf16[32,2048]{1,0:T(8,128)(2,1)S(1)}, u32[]{:S(2)}, u32[]{:S(2)}) collective-permute-start(bf16[32,2048]{1,0:T(8,128)(2,1)S(1)} %slice.68), channel_id=1, source_target_pairs={{0,1},{1,0},{2,3},{3,2},{4,5},{5,4},{6,7},{7,6},{8,9},{9,8},{10,11... | collective-permute-start | bytes 393224 | tf_op jit(solution)/shard_map/ppermute | solution.py:163
  41.2 4.5 %collective-permute-start.16 = (bf16[16,2048]{1,0:T(8,128)(2,1)S(1)}, bf16[16,2048]{1,0:T(8,128)(2,1)S(1)}, u32[]{:S(2)}, u32[]{:S(2)}) collective-permute-start(bf16[16,2048]{1,0:T(8,128)(2,1)S(1)} %slice.76), channel_id=1, source_target_pairs={{0,2},{1,3},{2,0},{3,1},{4,6},{5,7},{6,4},{7,5},{8,10},{9,11},{10,... | collective-permute-start | bytes 196616 | tf_op jit(solution)/shard_map/ppermute | solution.py:163
  42.5 7.5 %collective-permute-start.20 = (bf16[32,2048]{1,0:T(8,128)(2,1)S(1)}, bf16[32,2048]{1,0:T(8,128)(2,1)S(1)}, u32[]{:S(2)}, u32[]{:S(2)}) collective-permute-start(bf16[32,2048]{1,0:T(8,128)(2,1)S(1)} %add_convert_fusion), channel_id=1, source_target_pairs={{0,12},{1,13},{2,14},{3,15},{4,8},{5,9},{6,10},{7,11},{8,4},{9,5},... | collective-permute-start | bytes 393224 | tf_op jit(solution)/shard_map/ppermute | solution.py:163
  47.7 2.4 %collective-permute-start.17 = (bf16[32,2048]{1,0:T(8,128)(2,1)S(1)}, bf16[32,2048]{1,0:T(8,128)(2,1)S(1)}, u32[]{:S(2)}, u32[]{:S(2)}) collective-permute-start(bf16[32,2048]{1,0:T(8,128)(2,1)S(1)} %slice.66), channel_id=1, source_target_pairs={{0,1},{1,0},{2,3},{3,2},{4,5},{5,4},{6,7},{7,6},{8,9},{9,8},{10,11... | collective-permute-start | bytes 393224 | tf_op jit(solution)/shard_map/ppermute | solution.py:163
  47.7 6.6 %collective-permute-start.22 = (bf16[16,2048]{1,0:T(8,128)(2,1)S(1)}, bf16[16,2048]{1,0:T(8,128)(2,1)S(1)}, u32[]{:S(2)}, u32[]{:S(2)}) collective-permute-start(bf16[16,2048]{1,0:T(8,128)(2,1)S(1)} %add_convert_fusion.3), channel_id=1, source_target_pairs={{0,8},{1,9},{2,10},{3,11},{4,12},{5,13},{6,14},{7,15},{8,0},{9,1},... | collective-permute-start | bytes 196616 | tf_op jit(solution)/shard_map/ppermute | solution.py:163
  50.1 4.3 %collective-permute-start.21 = (bf16[16,2048]{1,0:T(8,128)(2,1)S(1)}, bf16[16,2048]{1,0:T(8,128)(2,1)S(1)}, u32[]{:S(2)}, u32[]{:S(2)}) collective-permute-start(bf16[16,2048]{1,0:T(8,128)(2,1)S(1)} %slice.92), channel_id=1, source_target_pairs={{0,2},{1,3},{2,0},{3,1},{4,6},{5,7},{6,4},{7,5},{8,10},{9,11},{10,... | collective-permute-start | bytes 196616 | tf_op jit(solution)/shard_map/ppermute | solution.py:163
